TPU v7x, 32 devices: a whole 2x2x4 slice. The times are simulated.
32 devices in a mesh: batch: 4 (over z), ctx: 2 (over y), head: 4 (over x, core).
Axes of the slice: x: 2, y: 2, z: 4, core: 2. Of those that a mesh axis runs over, the one named last changes fastest.
Arguments:
- tokens: bfloat16 [4, 1024, 640], P('batch', ('ctx', 'head')), may hold values from -6 to 6
- attn_in_gain: float32 [640], replicated, may hold values from 0.25 to 1.75
- query_weight: bfloat16 [640, 1024], P(None, ('batch', 'ctx')), may hold values from -0.25 to 0.25
- key_weight: bfloat16 [640, 256], P(None, ('batch', 'ctx')), may hold values from -0.25 to 0.25
- value_weight: bfloat16 [640, 256], P(None, ('batch', 'ctx')), may hold values from -0.25 to 0.25
- query_gain: float32 [256], replicated, may hold values from 0.25 to 1.75
- key_gain: float32 [256], replicated, may hold values from 0.25 to 1.75
- out_weight: bfloat16 [1024, 640], P(('batch', 'ctx')), may hold values from -0.1875 to 0.1875
- attn_out_gain: float32 [640], replicated, may hold values from 0.25 to 1.75
- ffn_in_gain: float32 [640], replicated, may hold values from 0.25 to 1.75
- gate_weight: bfloat16 [640, 2048], P(None, ('batch', 'ctx')), may hold values from -0.25 to 0.25
- up_weight: bfloat16 [640, 2048], P(None, ('batch', 'ctx')), may hold values from -0.25 to 0.25
- down_weight: bfloat16 [2048, 640], P(('batch', 'ctx')), may hold values from -0.125 to 0.125
- ffn_out_gain: float32 [640], replicated, may hold values from 0.25 to 1.75
- cotangent: bfloat16 [4, 1024, 640], P('batch', ('ctx', 'head')), may hold values from -6 to 6
Outputs:
- block_out: bfloat16 [4, 1024, 640], P('batch', ('ctx', 'head'))
- tokens_grad: float32 [4, 1024, 640], P('batch', ('ctx', 'head'))
- attn_in_gain_grad: float32 [640], replicated
- query_weight_grad: float32 [640, 1024], P(None, ('batch', 'ctx'))
- key_weight_grad: float32 [640, 256], P(None, ('batch', 'ctx'))
- value_weight_grad: float32 [640, 256], P(None, ('batch', 'ctx'))
- query_gain_grad: float32 [256], replicated
- key_gain_grad: float32 [256], replicated
- out_weight_grad: float32 [1024, 640], P(('batch', 'ctx'))
- attn_out_gain_grad: float32 [640], replicated
- ffn_in_gain_grad: float32 [640], replicated
- gate_weight_grad: float32 [640, 2048], P(None, ('batch', 'ctx'))
- up_weight_grad: float32 [640, 2048], P(None, ('batch', 'ctx'))
- down_weight_grad: float32 [2048, 640], P(('batch', 'ctx'))
- ffn_out_gain_grad: float32 [640], replicated
All inputs are finite; a program needn't handle non-finite values.
Results may differ from a plain program's by a relative error of at most 0.02.
Values may be sent and summed in bfloat16 or wider, within the bound.
A program may use at most 128 MiB of HBM per device.

v0:
```python
import math

import jax
import jax.numpy as jnp
from jax import lax
from jax.sharding import PartitionSpec as P

norm_eps = 1e-06
rope_base = 1000000.0


def rms_scale(values, gain):
    return values * lax.rsqrt(jnp.mean(values * values, axis=-1, keepdims=True) + norm_eps) * gain


def angles(positions, size):
    half_size = size // 2
    freq = jnp.exp(jnp.arange(half_size, dtype=jnp.float32) * (-2.0 * math.log(rope_base) / size))
    turned = positions[:, None] * freq[None, :]
    return (jnp.cos(turned), jnp.sin(turned))


def rotate(values, cosine, sine):
    half_size = values.shape[-1] // 2
    first = values[..., :half_size]
    second = values[..., half_size:]
    return jnp.concatenate(
        [first * cosine - second * sine, second * cosine + first * sine], axis=-1
    )


def geglu(gate_pre, up_pre):
    return jax.nn.gelu(gate_pre, approximate=True) * up_pre


def contract_rows(left, right):
    return lax.dot_general(
        left, right, (((0,), (0,)), ((), ())), preferred_element_type=jnp.float32
    )


def contract_cols(left, right):
    return lax.dot_general(
        left, right, (((1,), (1,)), ((), ())), preferred_element_type=jnp.float32
    )


def local(
    tokens,
    attn_in_gain,
    query_weight,
    key_weight,
    value_weight,
    query_gain,
    key_gain,
    out_weight,
    attn_out_gain,
    ffn_in_gain,
    gate_weight,
    up_weight,
    down_weight,
    ffn_out_gain,
    cotangent,
):
    heads = lax.axis_size("head")
    ctx_index = lax.axis_index("ctx")
    head_index = lax.axis_index("head")
    tok = tokens.shape[1]
    head_dim = key_gain.shape[0]
    scale = head_dim ** (-0.5)
    full_q, full_k, full_v, full_o, full_gate, full_up, full_down = (
        lax.all_gather(query_weight, ("batch", "ctx"), axis=1, tiled=True),
        lax.all_gather(key_weight, ("batch", "ctx"), axis=1, tiled=True),
        lax.all_gather(value_weight, ("batch", "ctx"), axis=1, tiled=True),
        lax.all_gather(out_weight, ("batch", "ctx"), axis=0, tiled=True),
        lax.all_gather(gate_weight, ("batch", "ctx"), axis=1, tiled=True),
        lax.all_gather(up_weight, ("batch", "ctx"), axis=1, tiled=True),
        lax.all_gather(down_weight, ("batch", "ctx"), axis=0, tiled=True),
    )
    inputs = tokens[0].astype(jnp.float32)
    first_pos = (ctx_index * heads + head_index) * tok
    positions = (first_pos + jnp.arange(tok, dtype=jnp.int32)).astype(jnp.float32)
    cosine, sine = angles(positions, head_dim)
    normed_f, pull_in = jax.vjp(rms_scale, inputs, attn_in_gain)
    normed_in = normed_f.astype(jnp.bfloat16)
    query_raw = jnp.dot(normed_in, full_q, preferred_element_type=jnp.float32).reshape(
        tok, heads, head_dim
    )
    key_raw = jnp.dot(normed_in, full_k, preferred_element_type=jnp.float32)
    value_low = jnp.dot(normed_in, full_v, preferred_element_type=jnp.float32).astype(jnp.bfloat16)

    def query_path(values, gain):
        return rotate(rms_scale(values, gain), cosine[:, None, :], sine[:, None, :])

    def key_path(values, gain):
        return rotate(rms_scale(values, gain), cosine, sine)

    query_rot, pull_query = jax.vjp(query_path, query_raw, query_gain)
    key_rot, pull_key = jax.vjp(key_path, key_raw, key_gain)
    query_low = query_rot.astype(jnp.bfloat16)
    key_low = key_rot.astype(jnp.bfloat16)
    query_heads = lax.all_to_all(query_low, "head", split_axis=1, concat_axis=0, tiled=True)[
        :, 0, :
    ]
    key_rows, value_rows = (
        lax.all_gather(key_low, ("ctx", "head"), axis=0, tiled=True),
        lax.all_gather(value_low, ("ctx", "head"), axis=0, tiled=True),
    )
    rows = query_heads.shape[0]
    query_pos = ctx_index * rows + jnp.arange(rows, dtype=jnp.int32)
    blocks_used = ctx_index + 1

    def block_scores(block):
        key_block = lax.dynamic_slice_in_dim(key_rows, block * rows, rows, 0)
        scores = contract_cols(query_heads, key_block) * scale
        key_pos = block * rows + jnp.arange(rows, dtype=jnp.int32)
        scores = jnp.where(key_pos[None, :] <= query_pos[:, None], scores, -jnp.inf)
        return (scores, key_block)

    def stats_step(block, carry):
        row_max, row_sum = carry
        scores, unused = block_scores(block)
        new_max = jnp.maximum(row_max, jnp.max(scores, axis=1))
        row_sum = row_sum * jnp.exp(row_max - new_max) + jnp.sum(
            jnp.exp(scores - new_max[:, None]), axis=1
        )
        return (new_max, row_sum)

    row_max, row_sum = lax.fori_loop(
        0,
        blocks_used,
        stats_step,
        (jnp.full((rows,), -jnp.inf, jnp.float32), jnp.zeros((rows,), jnp.float32)),
    )
    log_norm = row_max + jnp.log(row_sum)

    def output_step(block, acc):
        scores, unused = block_scores(block)
        probs = jnp.exp(scores - log_norm[:, None]).astype(jnp.bfloat16)
        value_block = lax.dynamic_slice_in_dim(value_rows, block * rows, rows, 0)
        return acc + jnp.dot(probs, value_block, preferred_element_type=jnp.float32)

    attended = lax.fori_loop(0, blocks_used, output_step, jnp.zeros((rows, head_dim), jnp.float32))
    attended_low = attended.astype(jnp.bfloat16)
    attended_tok = lax.all_to_all(
        attended_low[:, None, :], "head", split_axis=0, concat_axis=1, tiled=True
    ).reshape(tok, heads * head_dim)
    projected = jnp.dot(attended_tok, full_o, preferred_element_type=jnp.float32)
    post_attn, pull_aout = jax.vjp(rms_scale, projected, attn_out_gain)
    resid = inputs + post_attn
    normed_ffn_f, pull_fin = jax.vjp(rms_scale, resid, ffn_in_gain)
    normed_ffn = normed_ffn_f.astype(jnp.bfloat16)
    gate_pre = jnp.dot(normed_ffn, full_gate, preferred_element_type=jnp.float32)
    up_pre = jnp.dot(normed_ffn, full_up, preferred_element_type=jnp.float32)
    hidden_f, pull_glu = jax.vjp(geglu, gate_pre, up_pre)
    hidden = hidden_f.astype(jnp.bfloat16)
    mixed = jnp.dot(hidden, full_down, preferred_element_type=jnp.float32)
    post_ffn, pull_fout = jax.vjp(rms_scale, mixed, ffn_out_gain)
    block_out = (resid + post_ffn).astype(jnp.bfloat16)
    out_grad = cotangent[0].astype(jnp.float32)
    mixed_grad_f, fout_gain_grad = pull_fout(out_grad)
    mixed_grad = mixed_grad_f.astype(jnp.bfloat16)
    down_grad = contract_rows(hidden, mixed_grad)
    hidden_grad = contract_cols(mixed_grad, full_down)
    gate_grad_f, up_grad_f = pull_glu(hidden_grad)
    gate_grad = gate_grad_f.astype(jnp.bfloat16)
    up_grad = up_grad_f.astype(jnp.bfloat16)
    gate_w_grad = contract_rows(normed_ffn, gate_grad)
    up_w_grad = contract_rows(normed_ffn, up_grad)
    normed_ffn_grad = contract_cols(gate_grad, full_gate) + contract_cols(up_grad, full_up)
    resid_part, fin_gain_grad = pull_fin(normed_ffn_grad)
    resid_grad = out_grad + resid_part
    projected_grad_f, aout_gain_grad = pull_aout(resid_grad)
    projected_grad = projected_grad_f.astype(jnp.bfloat16)
    out_w_grad = contract_rows(attended_tok, projected_grad)
    attended_grad = (
        contract_cols(projected_grad, full_o).astype(jnp.bfloat16).reshape(tok, heads, head_dim)
    )
    grad_heads = lax.all_to_all(attended_grad, "head", split_axis=1, concat_axis=0, tiled=True)[
        :, 0, :
    ]
    delta = jnp.sum(grad_heads.astype(jnp.float32) * attended, axis=1)

    def backward_step(block, carry):
        query_acc, key_acc, value_acc = carry
        scores, key_block = block_scores(block)
        probs = jnp.exp(scores - log_norm[:, None])
        probs_low = probs.astype(jnp.bfloat16)
        value_block = lax.dynamic_slice_in_dim(value_rows, block * rows, rows, 0)
        probs_grad = contract_cols(grad_heads, value_block)
        score_grad = (probs * (probs_grad - delta[:, None])).astype(jnp.bfloat16)
        query_acc = (
            query_acc + jnp.dot(score_grad, key_block, preferred_element_type=jnp.float32) * scale
        )
        key_part = contract_rows(score_grad, query_heads) * scale
        value_part = contract_rows(probs_low, grad_heads)
        key_acc = lax.dynamic_update_slice_in_dim(key_acc, key_part, block * rows, 0)
        value_acc = lax.dynamic_update_slice_in_dim(value_acc, value_part, block * rows, 0)
        return (query_acc, key_acc, value_acc)

    seq_rows = key_rows.shape[0]
    query_acc, key_acc, value_acc = lax.fori_loop(
        0,
        blocks_used,
        backward_step,
        (
            jnp.zeros((rows, head_dim), jnp.float32),
            jnp.zeros((seq_rows, head_dim), jnp.float32),
            jnp.zeros((seq_rows, head_dim), jnp.float32),
        ),
    )
    key_low_grad, value_grad_f = (
        lax.psum_scatter(key_acc, ("ctx", "head"), scatter_dimension=0, tiled=True),
        lax.psum_scatter(value_acc, ("ctx", "head"), scatter_dimension=0, tiled=True),
    )
    query_low_grad = lax.all_to_all(
        query_acc.astype(jnp.bfloat16)[:, None, :], "head", split_axis=0, concat_axis=1, tiled=True
    )
    query_raw_grad_f, query_gain_grad = pull_query(query_low_grad.astype(jnp.float32))
    key_raw_grad_f, key_gain_grad = pull_key(key_low_grad)
    query_raw_grad = query_raw_grad_f.reshape(tok, heads * head_dim).astype(jnp.bfloat16)
    key_raw_grad = key_raw_grad_f.astype(jnp.bfloat16)
    value_grad = value_grad_f.astype(jnp.bfloat16)
    query_w_grad = contract_rows(normed_in, query_raw_grad)
    key_w_grad = contract_rows(normed_in, key_raw_grad)
    value_w_grad = contract_rows(normed_in, value_grad)
    normed_in_grad = (
        contract_cols(query_raw_grad, full_q)
        + contract_cols(key_raw_grad, full_k)
        + contract_cols(value_grad, full_v)
    )
    inputs_part, ain_gain_grad = pull_in(normed_in_grad)
    inputs_grad = resid_grad + inputs_part
    weight_grads = (
        query_w_grad,
        key_w_grad,
        value_w_grad,
        out_w_grad,
        gate_w_grad,
        up_w_grad,
        down_grad,
    )
    shards = (
        lax.psum_scatter(weight_grads[0], ("batch", "ctx"), scatter_dimension=1, tiled=True),
        lax.psum_scatter(weight_grads[1], ("batch", "ctx"), scatter_dimension=1, tiled=True),
        lax.psum_scatter(weight_grads[2], ("batch", "ctx"), scatter_dimension=1, tiled=True),
        lax.psum_scatter(weight_grads[3], ("batch", "ctx"), scatter_dimension=0, tiled=True),
        lax.psum_scatter(weight_grads[4], ("batch", "ctx"), scatter_dimension=1, tiled=True),
        lax.psum_scatter(weight_grads[5], ("batch", "ctx"), scatter_dimension=1, tiled=True),
        lax.psum_scatter(weight_grads[6], ("batch", "ctx"), scatter_dimension=0, tiled=True),
    )
    shards = (
        lax.psum(shards[0].astype(jnp.bfloat16), "head").astype(jnp.float32),
        lax.psum(shards[1].astype(jnp.bfloat16), "head").astype(jnp.float32),
        lax.psum(shards[2].astype(jnp.bfloat16), "head").astype(jnp.float32),
        lax.psum(shards[3].astype(jnp.bfloat16), "head").astype(jnp.float32),
        lax.psum(shards[4].astype(jnp.bfloat16), "head").astype(jnp.float32),
        lax.psum(shards[5].astype(jnp.bfloat16), "head").astype(jnp.float32),
        lax.psum(shards[6].astype(jnp.bfloat16), "head").astype(jnp.float32),
    )
    gains = lax.psum(
        (
            ain_gain_grad,
            query_gain_grad,
            key_gain_grad,
            aout_gain_grad,
            fin_gain_grad,
            fout_gain_grad,
        ),
        ("batch", "ctx", "head"),
    )
    return (
        block_out[None],
        inputs_grad[None],
        gains[0],
        shards[0],
        shards[1],
        shards[2],
        gains[1],
        gains[2],
        shards[3],
        gains[3],
        gains[4],
        shards[4],
        shards[5],
        shards[6],
        gains[5],
    )


def solution(mesh):
    in_specs = (
        P("batch", ("ctx", "head"), None),
        P(),
        P(None, ("batch", "ctx")),
        P(None, ("batch", "ctx")),
        P(None, ("batch", "ctx")),
        P(),
        P(),
        P(("batch", "ctx"), None),
        P(),
        P(),
        P(None, ("batch", "ctx")),
        P(None, ("batch", "ctx")),
        P(("batch", "ctx"), None),
        P(),
        P("batch", ("ctx", "head"), None),
    )
    out_specs = (
        P("batch", ("ctx", "head"), None),
        P("batch", ("ctx", "head"), None),
        P(),
        P(None, ("batch", "ctx")),
        P(None, ("batch", "ctx")),
        P(None, ("batch", "ctx")),
        P(),
        P(),
        P(("batch", "ctx"), None),
        P(),
        P(),
        P(None, ("batch", "ctx")),
        P(None, ("batch", "ctx")),
        P(("batch", "ctx"), None),
        P(),
    )
    return jax.shard_map(local, mesh=mesh, in_specs=in_specs, out_specs=out_specs, check_vma=False)
```

profile of v0, /device:TPU:9, one launch (start us, length us, event | category | flops | bytes accessed | tf_op | source)
XLA Modules:
  0.0 1059.6 jit_solution(17305379064022859422)
XLA Ops:
  10.7 22.7 %all_gather.27 = bf16[640,256]{0,1:T(8,128)(2,1)S(1)} all-gather(bf16[640,32]{0,1:T(8,128)(2,1)} %param.24), channel_id=1, replica_groups=mesh['batch'=4,'ctx'=2,'head'=4] {'batch','ctx'}, dimensions={1}, use_global_device_ids=true | all-gather | bytes 368640 | tf_op jit(solution)/shard_map/all_gather | solution.py:73
  33.4 1.1 fusion.66
  34.5 1.3 multiply_reduce_fusion.13
  35.9 25.6 %all_gather.30 = bf16[640,256]{0,1:T(8,128)(2,1)S(1)} all-gather(bf16[640,32]{0,1:T(8,128)(2,1)} %param.25), channel_id=1, replica_groups=mesh['batch'=4,'ctx'=2,'head'=4] {'batch','ctx'}, dimensions={1}, use_global_device_ids=true | all-gather | bytes 368640 | tf_op jit(solution)/shard_map/all_gather | solution.py:74
  63.0 1.7 copy.43
  66.4 15.9 %all-to-all-start = ((bf16[128,4,256]{2,0,1:T(8,128)(2,1)}), bf16[128,4,256]{2,0,1:T(8,128)(2,1)S(1)}, u32[]{:S(2)}, u32[]{:S(2)}) async-start(bf16[128,4,256]{2,0,1:T(8,128)(2,1)} %pad_maximum_fusion), calls=%async_computation | async-start | bytes 524288 | tf_op jit(solution)/shard_map/all_to_all | solution.py:102
  82.3 12.5 %all_gather.28 = bf16[1024,256]{1,0:T(8,128)(2,1)S(1)} all-gather(bf16[128,256]{1,0:T(8,128)(2,1)S(1)} %pad_maximum_fusion.1), channel_id=1, replica_groups=mesh['batch'=4,'ctx'=2,'head'=4] {'ctx','head'}, dimensions={0}, use_global_device_ids=true | all-gather | bytes 589824 | tf_op jit(solution)/shard_map/all_gather | solution.py:106
  94.8 9.8 all_gather.31
  107.7 7.5 all_to_all.54
  115.8 1.9 multiply_reduce_fusion.10
  118.0 36.9 %all-gather.10.cloned.1.call-done = bf16[640,2048]{1,0:T(8,128)(2,1)} async-done(((bf16[640,256]{1,0:T(8,128)(2,1)}), bf16[640,2048]{1,0:T(8,128)(2,1)}) %all-gather.10.cloned.1.call-update) | async-done | bytes 2621456 | tf_op jit(solution)/shard_map/all_gather | solution.py:76
  154.9 3.3 fusion.114
  158.2 53.7 %all-gather.12.cloned.1.call-done = bf16[640,2048]{1,0:T(8,128)(2,1)} async-done(((bf16[640,256]{1,0:T(8,128)(2,1)}), bf16[640,2048]{1,0:T(8,128)(2,1)}) %all-gather.12.cloned.1.call-update) | async-done | bytes 2621456 | tf_op jit(solution)/shard_map/all_gather | solution.py:77
  211.9 3.8 multiply_convert_fusion.1
  215.7 52.2 %all-gather.14.cloned.1.call-done = bf16[2048,640]{1,0:T(8,128)(2,1)} async-done(((bf16[256,640]{1,0:T(8,128)(2,1)}), bf16[2048,640]{1,0:T(8,128)(2,1)}) %all-gather.14.cloned.1.call-update) | async-done | bytes 2621456 | tf_op jit(solution)/shard_map/all_gather | solution.py:78
  267.9 2.6 multiply_reduce_fusion.8
  272.2 1.4 multiply_convert_fusion
  273.9 0.9 fusion.115
  274.8 0.9 copy-done.1
  275.8 1.1 multiply_reduce_fusion.4
  279.4 5.2 all-to-all-start.2
  284.6 5.2 all-to-all-done.2
  289.8 1.2 multiply_reduce_fusion.2
  291.0 1.0 broadcast.282
  292.0 1.0 broadcast.282.clone
  293.1 3.0 while.41
  297.0 36.1 %reduce-scatter.10.cloned.1.call-done = f32[128,256]{1,0:T(8,128)} async-done(((f32[1024,256]{1,0:T(8,128)}), f32[128,256]{1,0:T(8,128)}) %reduce-scatter.10.cloned.1.call-update) | async-done | bytes 131088 | tf_op jit(solution)/shard_map/reduce_scatter | solution.py:213
  333.1 1.2 fusion.93
  334.3 1.0 multiply_reduce_fusion.11
  335.5 1.2 fusion.107
  336.8 35.6 %reduce-scatter.12.cloned.1.call-done = f32[128,256]{1,0:T(8,128)} async-done(((f32[1024,256]{1,0:T(8,128)}), f32[128,256]{1,0:T(8,128)}) %reduce-scatter.12.cloned.1.call-update) | async-done | bytes 131088 | tf_op jit(solution)/shard_map/reduce_scatter | solution.py:214
  372.4 2.1 fusion.97
  374.5 2.0 fusion.117
  377.5 8.3 all_to_all.55
  386.9 2.1 fusion.78
  389.1 3.2 fusion.118
  392.4 1.0 copy-done.17
  393.4 3.3 fusion.119
  397.6 3.2 fusion.120
  400.8 1.2 copy-done.3
  402.6 33.8 %reduce-scatter.16.cloned.1.call-done = f32[640,32]{0,1:T(8,128)} async-done(((f32[640,256]{0,1:T(8,128)}), f32[640,32]{0,1:T(8,128)}) %reduce-scatter.16.cloned.1.call-update) | async-done | bytes 81936 | tf_op jit(solution)/shard_map/reduce_scatter | solution.py:245
  436.4 1.5 convert_element_type.177
  437.9 63.9 %reduce-scatter.18.cloned.1.call-done = f32[640,32]{0,1:T(8,128)} async-done(((f32[640,256]{0,1:T(8,128)}), f32[640,32]{0,1:T(8,128)}) %reduce-scatter.18.cloned.1.call-update) | async-done | bytes 81936 | tf_op jit(solution)/shard_map/reduce_scatter | solution.py:246
  501.8 1.5 convert_element_type.179
  503.6 71.4 %reduce-scatter.20.cloned.1.call-done = f32[128,640]{1,0:T(8,128)} async-done(((f32[1024,640]{1,0:T(8,128)}), f32[128,640]{1,0:T(8,128)}) %reduce-scatter.20.cloned.1.call-update) | async-done | bytes 327696 | tf_op jit(solution)/shard_map/reduce_scatter | solution.py:247
  575.0 1.7 convert_element_type.181
  576.6 71.8 %reduce-scatter.14.cloned.1.call-done = f32[640,128]{1,0:T(8,128)} async-done(((f32[640,1024]{1,0:T(8,128)}), f32[640,128]{1,0:T(8,128)}) %reduce-scatter.14.cloned.1.call-update) | async-done | bytes 327696 | tf_op jit(solution)/shard_map/reduce_scatter | solution.py:244
  648.4 1.7 convert_element_type.175
  650.1 105.2 %reduce-scatter.22.cloned.1.call-done = f32[640,256]{1,0:T(8,128)} async-done(((f32[640,2048]{1,0:T(8,128)}), f32[640,256]{1,0:T(8,128)}) %reduce-scatter.22.cloned.1.call-update) | async-done | bytes 655376 | tf_op jit(solution)/shard_map/reduce_scatter | solution.py:248
  755.3 1.8 convert_element_type.183
  757.1 104.5 %reduce-scatter.24.cloned.1.call-done = f32[640,256]{1,0:T(8,128)} async-done(((f32[640,2048]{1,0:T(8,128)}), f32[640,256]{1,0:T(8,128)}) %reduce-scatter.24.cloned.1.call-update) | async-done | bytes 655376 | tf_op jit(solution)/shard_map/reduce_scatter | solution.py:249
  861.6 1.8 convert_element_type.185
  863.5 103.9 %reduce-scatter.26.cloned.1.call-done = f32[256,640]{1,0:T(8,128)} async-done(((f32[2048,640]{1,0:T(8,128)}), f32[256,640]{1,0:T(8,128)}) %reduce-scatter.26.cloned.1.call-update) | async-done | bytes 655376 | tf_op jit(solution)/shard_map/reduce_scatter | solution.py:250
  967.4 1.8 convert_element_type.187
  969.6 39.5 %all-reduce.4 = (f32[640]{0:T(1024)}, f32[256]{0:T(256)}, f32[256]{0:T(256)}, f32[640]{0:T(1024)}, f32[640]{0:T(1024)}, /*index=5*/f32[640]{0:T(1024)}) all-reduce(f32[640]{0:T(1024)S(1)} %get-tuple-element.242, f32[256]{0:T(256)S(1)} %get-tuple-element.234, ...), channel_id=1, replica_groups=mesh['batch'=4,'ctx'=2,'head'=4] {'batch','ctx','head'}, use_global_device_ids=true, to_apply=%region_24.25 | all-reduce | flops 3072 | bytes 24576 | tf_op jit(solution)/shard_map/psum | solution.py:261
  1009.1 0.9 fusion.73
  1010.0 1.4 convert_element_type.178
  1011.4 1.4 convert_element_type.180
  1012.8 32.3 %all-reduce.12.cloned.1.call-done = (bf16[640,128]{1,0:T(8,128)(2,1)}, bf16[128,640]{1,0:T(8,128)(2,1)}, bf16[640,256]{1,0:T(8,128)(2,1)}, bf16[640,256]{1,0:T(8,128)(2,1)}, bf16[256,640]{1,0:T(8,128)(2,1)}) async-done(((bf16[640,128]{1,0:T(8,128)(2,1)}, bf16[128,640]{1,0:T(8,128)(2,1)}, bf16[640,256]{1,0:T(8,128)(2,1)}, bf16[640,256]{1,0:T(8,128)(2,1)}, bf16[256,640]{1,0:T(8,128)(2,1)}), ...) | async-done | bytes 1310736 | tf_op jit(solution)/shard_map/psum | solution.py:253
  1045.2 1.7 convert_element_type.176
  1046.9 1.7 convert_element_type.182
  1048.5 1.9 convert_element_type.184
  1050.4 1.9 convert_element_type.186
  1052.2 0.9 convert_element_type.188
  (228 shorter events, 24.4 us)
Async XLA Ops:
  7.2 55.0 %copy-start.2 = (bf16[1,128,640]{2,1,0:T(8,128)(2,1)S(1)}, bf16[1,128,640]{2,1,0:T(8,128)(2,1)}, u32[]{:S(2)}) copy-start(bf16[1,128,640]{2,1,0:T(8,128)(2,1)} %param.21) | copy-start | bytes 491524
  7.2 55.0 %copy-start.38 = (f32[640]{0:T(1024)S(1)}, f32[640]{0:T(1024)}, u32[]{:S(2)}) copy-start(f32[640]{0:T(1024)} %param.22) | copy-start | bytes 7684
  7.2 55.2 %copy-start.46 = (f32[256]{0:T(256)S(1)}, f32[256]{0:T(256)}, u32[]{:S(2)}) copy-start(f32[256]{0:T(256)} %param.27) | copy-start | bytes 3076
  7.2 55.7 %all-gather.6.cloned.1.call-start = ((), (), s32[]{:S(2)}) async-start(), calls=%async_computation.13 | async-start | bytes 1474560 | tf_op jit(solution)/shard_map/all_gather | solution.py:72
  7.9 107.8 %all-gather.8.cloned.1.call-start = ((), (), s32[]{:S(2)}) async-start(), calls=%async_computation.14 | async-start | bytes 1474560 | tf_op jit(solution)/shard_map/all_gather | solution.py:75
  8.7 146.2 %all-gather.10.cloned.1.call-start = ((), (), s32[]{:S(2)}) async-start(), calls=%async_computation.15 | async-start | bytes 2949120 | tf_op jit(solution)/shard_map/all_gather | solution.py:76
  9.4 202.4 %all-gather.12.cloned.1.call-start = ((), (), s32[]{:S(2)}) async-start(), calls=%async_computation.16 | async-start | bytes 2949120 | tf_op jit(solution)/shard_map/all_gather | solution.py:77
  10.0 257.9 %all-gather.14.cloned.1.call-start = ((), (), s32[]{:S(2)}) async-start(), calls=%async_computation.17 | async-start | bytes 2949120 | tf_op jit(solution)/shard_map/all_gather | solution.py:78
  10.6 54.1 %copy-start.52 = (f32[128]{0:T(128)}, f32[128]{0:T(128)S(1)}, u32[]{:S(2)}) copy-start(f32[128]{0:T(128)S(1)} %multiply_exponential_fusion) | copy-start | bytes 1540
  10.6 54.0 %copy-start.54 = (f32[128]{0:T(128)}, f32[128]{0:T(128)S(1)}, u32[]{:S(2)}) copy-start(f32[128]{0:T(128)S(1)} %add_convert_fusion.2) | copy-start | bytes 1540
  33.4 31.3 %copy-start.23 = (bf16[640,256]{0,1:T(8,128)(2,1)}, bf16[640,256]{0,1:T(8,128)(2,1)S(1)}, u32[]{:S(2)}) copy-start(bf16[640,256]{0,1:T(8,128)(2,1)S(1)} %all_gather.27) | copy-start | bytes 983044
  34.5 30.2 %copy-start.58 = (f32[128]{0:T(128)}, f32[128]{0:T(128)S(1)}, u32[]{:S(2)}) copy-start(f32[128]{0:T(128)S(1)} %fusion.66) | copy-start | bytes 1540
  34.5 30.9 %copy-start.41 = (f32[128]{0:T(128)}, f32[128]{0:T(128)S(1)}, u32[]{:S(2)}) copy-start(f32[128]{0:T(128)S(1)} %fusion.101) | copy-start | bytes 1540
  35.8 28.9 %copy-start.27 = (f32[128,256]{1,0:T(8,128)}, f32[128,256]{1,0:T(8,128)S(1)}, u32[]{:S(2)}) copy-start(f32[128,256]{1,0:T(8,128)S(1)} %get-tuple-element.341) | copy-start | bytes 393220
  35.8 28.9 %copy-start.60 = (f32[128]{0:T(128)}, f32[128]{0:T(128)S(1)}, u32[]{:S(2)}) copy-start(f32[128]{0:T(128)S(1)} %get-tuple-element.340) | copy-start | bytes 1540
  35.8 28.9 %copy-start.50 = (f32[128]{0:T(128)}, f32[128]{0:T(128)S(1)}, u32[]{:S(2)}) copy-start(f32[128]{0:T(128)S(1)} %fusion.102) | copy-start | bytes 1540
  62.5 3.0 copy-start.48
  62.9 2.7 copy-start.32
  62.9 2.7 copy-start.34
  65.4 39.3 %copy-start.43 = (f32[128,4]{0,1:T(4,128)}, f32[128,4]{0,1:T(4,128)S(1)}, u32[]{:S(2)}) copy-start(f32[128,4]{0,1:T(4,128)S(1)} %get-tuple-element.342) | copy-start | bytes 6148
  66.4 38.2 %all-to-all-start = ((bf16[128,4,256]{2,0,1:T(8,128)(2,1)}), bf16[128,4,256]{2,0,1:T(8,128)(2,1)S(1)}, u32[]{:S(2)}, u32[]{:S(2)}) async-start(bf16[128,4,256]{2,0,1:T(8,128)(2,1)} %pad_maximum_fusion), calls=%async_computation | async-start | bytes 524288 | tf_op jit(solution)/shard_map/all_to_all | solution.py:102
  106.2 11.5 %copy-start.5 = (f32[512,256]{1,0:T(8,128)}, f32[512,256]{1,0:T(8,128)S(1)}, u32[]{:S(2)}) copy-start(f32[512,256]{1,0:T(8,128)S(1)} %get-tuple-element.164) | copy-start | bytes 1572868
  107.6 10.1 copy-start.40
  107.7 10.2 copy-start.39
  215.7 54.8 %copy-start.22 = (bf16[1,128,640]{2,1,0:T(8,128)(2,1)S(1)}, bf16[1,128,640]{2,1,0:T(8,128)(2,1)}, u32[]{:S(2)}) copy-start(bf16[1,128,640]{2,1,0:T(8,128)(2,1)} %param.35) | copy-start | bytes 491524
  215.7 54.8 %copy-start.45 = (f32[640]{0:T(1024)S(1)}, f32[640]{0:T(1024)}, u32[]{:S(2)}) copy-start(f32[640]{0:T(1024)} %param.34) | copy-start | bytes 7684
  267.9 4.3 copy-start.10
  267.9 4.3 copy-start.13
  267.9 4.3 copy-start.29
  273.5 3.3 copy-start.16
  273.5 3.3 copy-start.18
  275.8 2.3 copy-start.4
  278.7 14.4 %copy-start.57 = (f32[512]{0:T(512)S(1)}, f32[512]{0:T(512)}, u32[]{:S(2)}) copy-start(f32[512]{0:T(512)} %copy-done.56) | copy-start | bytes 6148
  279.4 10.4 all-to-all-start.2
  284.6 48.5 %reduce-scatter.10.cloned.1.call-start = ((), (), s32[]{:S(2)}) async-start(), calls=%async_computation.18 | async-start | bytes 1179648 | tf_op jit(solution)/shard_map/reduce_scatter | solution.py:213
  293.1 40.0 %copy-start.53 = (f32[128]{0:T(128)S(1)}, f32[128]{0:T(128)}, u32[]{:S(2)}) copy-start(f32[128]{0:T(128)} %copy-done.52) | copy-start | bytes 1540
  293.1 40.0 %copy-start.55 = (f32[128]{0:T(128)S(1)}, f32[128]{0:T(128)}, u32[]{:S(2)}) copy-start(f32[128]{0:T(128)} %copy-done.54) | copy-start | bytes 1540
  293.1 41.2 %copy-start.47 = (f32[256]{0:T(256)S(1)}, f32[256]{0:T(256)}, u32[]{:S(2)}) copy-start(f32[256]{0:T(256)} %param.27) | copy-start | bytes 3076
  293.1 41.2 %copy-start.51 = (f32[128]{0:T(128)S(1)}, f32[128]{0:T(128)}, u32[]{:S(2)}) copy-start(f32[128]{0:T(128)} %copy-done.50) | copy-start | bytes 1540
  296.2 39.2 %copy-start.61 = (f32[128]{0:T(128)S(1)}, f32[128]{0:T(128)}, u32[]{:S(2)}) copy-start(f32[128]{0:T(128)} %copy-done.60) | copy-start | bytes 1540
  296.2 39.3 %copy-start.28 = (f32[128,256]{1,0:T(8,128)S(1)}, f32[128,256]{1,0:T(8,128)}, u32[]{:S(2)}) copy-start(f32[128,256]{1,0:T(8,128)} %copy-done.27) | copy-start | bytes 393220
  296.2 39.4 %copy-start.42 = (f32[128]{0:T(128)S(1)}, f32[128]{0:T(128)}, u32[]{:S(2)}) copy-start(f32[128]{0:T(128)} %copy-done.41) | copy-start | bytes 1540
  296.2 78.3 %copy-start.15 = (bf16[128,4,1,256]{0,3,1,2:T(8,128)(2,1)S(1)}, bf16[128,4,1,256]{0,3,1,2:T(8,128)(2,1)}, u32[]{:S(2)}) copy-start(bf16[128,4,1,256]{0,3,1,2:T(8,128)(2,1)} %copy-done.14) | copy-start | bytes 786436
  296.2 78.3 %copy-start.21 = (bf16[128,640]{1,0:T(8,128)(2,1)S(1)}, bf16[128,640]{1,0:T(8,128)(2,1)}, u32[]{:S(2)}) copy-start(bf16[128,640]{1,0:T(8,128)(2,1)} %copy-done.20) | copy-start | bytes 491524
  296.2 76.2 %reduce-scatter.12.cloned.1.call-start = ((), (), s32[]{:S(2)}) async-start(), calls=%async_computation.19 | async-start | bytes 1179648 | tf_op jit(solution)/shard_map/reduce_scatter | solution.py:214
  297.0 139.4 %reduce-scatter.16.cloned.1.call-start = ((), (), s32[]{:S(2)}) async-start(), calls=%async_computation.21 | async-start | bytes 737280 | tf_op jit(solution)/shard_map/reduce_scatter | solution.py:245
  336.7 165.0 %reduce-scatter.18.cloned.1.call-start = ((), (), s32[]{:S(2)}) async-start(), calls=%async_computation.22 | async-start | bytes 737280 | tf_op jit(solution)/shard_map/reduce_scatter | solution.py:246
  374.4 200.5 %reduce-scatter.20.cloned.1.call-start = ((), (), s32[]{:S(2)}) async-start(), calls=%async_computation.23 | async-start | bytes 2949120 | tf_op jit(solution)/shard_map/reduce_scatter | solution.py:247
  376.5 9.7 copy-start.33
  376.5 9.7 copy-start.35
  376.5 271.9 %reduce-scatter.14.cloned.1.call-start = ((), (), s32[]{:S(2)}) async-start(), calls=%async_computation.20 | async-start | bytes 2949120 | tf_op jit(solution)/shard_map/reduce_scatter | solution.py:244
  376.6 9.7 copy-start.49
  377.5 9.1 copy-start.44
  389.1 366.2 %reduce-scatter.22.cloned.1.call-start = ((), (), s32[]{:S(2)}) async-start(), calls=%async_computation.24 | async-start | bytes 5898240 | tf_op jit(solution)/shard_map/reduce_scatter | solution.py:248
  392.4 469.3 %reduce-scatter.24.cloned.1.call-start = ((), (), s32[]{:S(2)}) async-start(), calls=%async_computation.25 | async-start | bytes 5898240 | tf_op jit(solution)/shard_map/reduce_scatter | solution.py:249
  396.7 570.8 %reduce-scatter.26.cloned.1.call-start = ((), (), s32[]{:S(2)}) async-start(), calls=%async_computation.26 | async-start | bytes 5898240 | tf_op jit(solution)/shard_map/reduce_scatter | solution.py:250
  400.7 102.6 %copy-start.24 = (bf16[640,256]{0,1:T(8,128)(2,1)S(1)}, bf16[640,256]{0,1:T(8,128)(2,1)}, u32[]{:S(2)}) copy-start(bf16[640,256]{0,1:T(8,128)(2,1)} %copy-done.23) | copy-start | bytes 983044
  400.7 609.2 %all-reduce.10.cloned.1.call-start = ((), (), s32[]{:S(2)}) async-start(), calls=%async_computation.27 | async-start | bytes 163840 | tf_op jit(solution)/shard_map/psum | solution.py:254
  503.3 541.9 %all-reduce.12.cloned.1.call-start = ((), (), s32[]{:S(2)}) async-start(), calls=%async_computation.28 | async-start | bytes 2621440 | tf_op jit(solution)/shard_map/psum | solution.py:253
  503.6 465.7 %copy-start.26 = (bf16[640,256]{0,1:T(8,128)(2,1)S(1)}, bf16[640,256]{0,1:T(8,128)(2,1)}, u32[]{:S(2)}) copy-start(bf16[640,256]{0,1:T(8,128)(2,1)} %copy-done.25) | copy-start | bytes 983044
  503.6 465.7 %copy-start.36 = (f32[128,256]{1,0:T(8,128)S(1)}, f32[128,256]{1,0:T(8,128)}, u32[]{:S(2)}) copy-start(f32[128,256]{1,0:T(8,128)} %reduce-scatter.12.cloned.1.call-done) | copy-start | bytes 393220
  650.1 359.1 %copy-start.59 = (f32[128]{0:T(128)S(1)}, f32[128]{0:T(128)}, u32[]{:S(2)}) copy-start(f32[128]{0:T(128)} %copy-done.58) | copy-start | bytes 1540
  650.1 359.1 %copy-start.12 = (f32[128,640]{1,0:T(8,128)S(1)}, f32[128,640]{1,0:T(8,128)}, u32[]{:S(2)}) copy-start(f32[128,640]{1,0:T(8,128)} %copy-done.11) | copy-start | bytes 983044
  1045.2 7.1 copy-start.37
  (16 other events, 20.1 us)
Sparse Core Ops, SparseCore 0:
  10.1 43.7 all-gather.5
  56.1 42.2 all-gather.7
  100.4 54.4 all-gather.9
  156.8 55.0 all-gather.11
  213.9 53.9 all-gather.13
  296.3 36.7 reduce-scatter.9
  336.3 36.0 reduce-scatter.11
  376.2 60.1 reduce-scatter.15
  440.6 61.1 reduce-scatter.17
  505.1 69.7 reduce-scatter.19
  578.5 69.8 reduce-scatter.13
  651.9 103.3 reduce-scatter.21
  758.9 102.7 reduce-scatter.23
  865.1 102.3 reduce-scatter.25
  970.2 30.2 all-reduce.9
  1004.4 40.7 all-reduce.11
where the time goes:
time: 1060 us
  waiting for transfers between devices  810 us (76%)
  blocking collectives  126 us (12%)
  matrix products  38.4 us (4%)
  other arithmetic  33.8 us (3%)
  starting transfers between devices  21.7 us (2%)
  between operations  14.9 us (1%)
  local copies, waits for them, and re-layouts  14.2 us (1%)
    reduce_scatter x1, waiting for transfers between devices, local(): lax.psum_scatter(weight_grads[4], ('batch', 'ctx'), scatter_dimension=1,...  105 us
    reduce_scatter x1, waiting for transfers between devices, local(): lax.psum_scatter(weight_grads[5], ('batch', 'ctx'), scatter_dimension=1,...  105 us
    reduce_scatter x1, waiting for transfers between devices, local(): lax.psum_scatter(weight_grads[6], ('batch', 'ctx'), scatter_dimension=0,...  104 us
    reduce_scatter x1, waiting for transfers between devices, local(): lax.psum_scatter(weight_grads[0], ('batch', 'ctx'), scatter_dimension=1,...  71.8 us
    reduce_scatter x1, waiting for transfers between devices, local(): lax.psum_scatter(weight_grads[3], ('batch', 'ctx'), scatter_dimension=0,...  71.4 us
    reduce_scatter x1, waiting for transfers between devices, local(): lax.psum_scatter(weight_grads[2], ('batch', 'ctx'), scatter_dimension=1,...  63.9 us
    all_gather x1, waiting for transfers between devices, local(): lax.all_gather(up_weight, ('batch', 'ctx'), axis=1, tiled=True)  53.7 us
    all_gather x1, waiting for transfers between devices, local(): lax.all_gather(down_weight, ('batch', 'ctx'), axis=0, tiled=True)  52.2 us
  transfers between devices with their start and end apart: 18, of which 14 were waited for; matrix products, arithmetic and copies ran while one was open for 5% of the time, Pallas kernels for 0%

commit v1 on v0

v1 whole, which is shorter than its diff:
```python
import functools
import math

import jax
import jax.numpy as jnp
from jax import lax
from jax.experimental import pallas as pl
from jax.experimental.pallas import tpu as pltpu
from jax.sharding import PartitionSpec as P

norm_eps = 1e-06
rope_base = 1000000.0


def rms_scale(values, gain):
    return values * lax.rsqrt(jnp.mean(values * values, axis=-1, keepdims=True) + norm_eps) * gain


def angles(positions, size):
    half_size = size // 2
    freq = jnp.exp(jnp.arange(half_size, dtype=jnp.float32) * (-2.0 * math.log(rope_base) / size))
    turned = positions[:, None] * freq[None, :]
    return (jnp.cos(turned), jnp.sin(turned))


def rotate(values, cosine, sine):
    half_size = values.shape[-1] // 2
    first = values[..., :half_size]
    second = values[..., half_size:]
    return jnp.concatenate(
        [first * cosine - second * sine, second * cosine + first * sine], axis=-1
    )


def geglu(gate_pre, up_pre):
    return jax.nn.gelu(gate_pre, approximate=True) * up_pre


def contract_rows(left, right):
    return lax.dot_general(
        left, right, (((0,), (0,)), ((), ())), preferred_element_type=jnp.float32
    )


def contract_cols(left, right):
    return lax.dot_general(
        left, right, (((1,), (1,)), ((), ())), preferred_element_type=jnp.float32
    )


vmem_limit = 52 * 1024 * 1024


def greet(axes):
    barrier = pltpu.get_barrier_semaphore()
    count = 0
    for axis in axes:
        size = lax.axis_size(axis)
        me = lax.axis_index(axis)
        for step in range(1, size):
            pl.semaphore_signal(
                barrier,
                inc=1,
                device_id={axis: lax.rem(me + step, size)},
                device_id_type=pl.DeviceIdType.MESH,
            )
            count += 1
    pl.semaphore_wait(barrier, count)


def send(source, target, send_sem, recv_sem, axis, index):
    copy = pltpu.make_async_remote_copy(
        src_ref=source,
        dst_ref=target,
        send_sem=send_sem,
        recv_sem=recv_sem,
        device_id={axis: index},
        device_id_type=pl.DeviceIdType.MESH,
    )
    copy.start()
    return copy


def gather_kernel(first, second, x_ref, out_ref, own_sem, send_a, recv_a, send_b, recv_b):
    size_a, size_b = lax.axis_size(first), lax.axis_size(second)
    at_a, at_b = lax.axis_index(first), lax.axis_index(second)
    greet((first, second))
    own = out_ref.at[at_a, at_b]
    sent_a, sent_b = [], []
    for step in range(1, size_a):
        sent_a.append(
            send(x_ref, own, send_a.at[step - 1], recv_a.at[step - 1], first,
                 lax.rem(at_a + step, size_a))
        )
    for turn in range(1, size_b):
        sent_b.append(
            send(x_ref, own, send_b.at[turn - 1, 0], recv_b.at[turn - 1, 0], second,
                 lax.rem(at_b + turn, size_b))
        )
    keep = pltpu.make_async_copy(x_ref, own, own_sem)
    keep.start()
    for step in range(1, size_a):
        sent_a[step - 1].wait_recv()
        slot = out_ref.at[lax.rem(at_a + size_a - step, size_a), at_b]
        for turn in range(1, size_b):
            sent_b.append(
                send(slot, slot, send_b.at[turn - 1, step], recv_b.at[turn - 1, step], second,
                     lax.rem(at_b + turn, size_b))
            )
    for copy in sent_b:
        copy.wait_recv()
    for copy in sent_a + sent_b:
        copy.wait_send()
    keep.wait()


def gather(values, first, second, number):
    size_a, size_b = lax.axis_size(first), lax.axis_size(second)
    dma = pltpu.SemaphoreType.DMA
    return pl.pallas_call(
        functools.partial(gather_kernel, first, second),
        out_shape=jax.ShapeDtypeStruct((size_a, size_b) + values.shape, values.dtype),
        in_specs=[pl.BlockSpec(memory_space=pl.ANY)],
        out_specs=pl.BlockSpec(memory_space=pl.ANY),
        scratch_shapes=[
            dma,
            dma((size_a - 1,)),
            dma((size_a - 1,)),
            dma((size_b - 1, size_a)),
            dma((size_b - 1, size_a)),
        ],
        compiler_params=pltpu.CompilerParams(
            collective_id=number, has_side_effects=True, vmem_limit_bytes=vmem_limit
        ),
        name="gather_" + first + "_" + second,
    )(values)


def scatter_kernel(
    first, second, x_ref, out_ref, held_b, part, held_a, send_a, recv_a, send_b, recv_b
):
    size_a, size_b = lax.axis_size(first), lax.axis_size(second)
    at_a, at_b = lax.axis_index(first), lax.axis_index(second)
    greet((first, second))
    order = list(range(1, size_a)) + [0]
    sent_a, sent_b = {}, {}
    for step in order:
        goal = lax.rem(at_a + step, size_a)
        for turn in range(1, size_b):
            other = lax.rem(at_b + turn, size_b)
            sent_b[turn, step] = send(
                x_ref.at[goal, other], held_b.at[turn - 1, step],
                send_b.at[turn - 1, step], recv_b.at[turn - 1, step], second, other,
            )
    for step in order:
        goal = lax.rem(at_a + step, size_a)
        total = x_ref[goal, at_b].astype(jnp.float32)
        for turn in range(1, size_b):
            sent_b[turn, step].wait_recv()
            total += held_b[turn - 1, step].astype(jnp.float32)
        if step > 0:
            part[step - 1] = total.astype(part.dtype)
            sent_a[step] = send(
                part.at[step - 1], held_a.at[step - 1],
                send_a.at[step - 1], recv_a.at[step - 1], first, goal,
            )
        else:
            for back in range(1, size_a):
                sent_a[back].wait_recv()
                total += held_a[back - 1].astype(jnp.float32)
            out_ref[...] = total.astype(out_ref.dtype)
    for copy in list(sent_a.values()) + list(sent_b.values()):
        copy.wait_send()


def scatter_sum(values, first, second, number, dtype=jnp.float32):
    size_a, size_b = lax.axis_size(first), lax.axis_size(second)
    block = values.shape[2:]
    dma = pltpu.SemaphoreType.DMA
    return pl.pallas_call(
        functools.partial(scatter_kernel, first, second),
        out_shape=jax.ShapeDtypeStruct(block, dtype),
        in_specs=[pl.BlockSpec(memory_space=pltpu.VMEM)],
        out_specs=pl.BlockSpec(memory_space=pltpu.VMEM),
        scratch_shapes=[
            pltpu.VMEM((size_b - 1, size_a) + block, values.dtype),
            pltpu.VMEM((size_a - 1,) + block, values.dtype),
            pltpu.VMEM((size_a - 1,) + block, values.dtype),
            dma((size_a - 1,)),
            dma((size_a - 1,)),
            dma((size_b - 1, size_a)),
            dma((size_b - 1, size_a)),
        ],
        compiler_params=pltpu.CompilerParams(
            collective_id=number, has_side_effects=True, vmem_limit_bytes=vmem_limit
        ),
        name="scatter_" + first + "_" + second,
    )(values)


def total_kernel(axis, x_ref, out_ref, held, send_a, recv_a, send_b, recv_b):
    size = lax.axis_size(axis)
    me = lax.axis_index(axis)
    greet((axis,))
    sent = []
    for step in range(1, size):
        other = lax.rem(me + step, size)
        sent.append(
            send(x_ref.at[other], held.at[step - 1], send_a.at[step - 1], recv_a.at[step - 1],
                 axis, other)
        )
    total = x_ref[me].astype(jnp.float32)
    for step in range(1, size):
        sent[step - 1].wait_recv()
        total += held[step - 1].astype(jnp.float32)
    out_ref[me] = total.astype(out_ref.dtype)
    again = []
    for step in range(1, size):
        again.append(
            send(out_ref.at[me], out_ref.at[me], send_b.at[step - 1], recv_b.at[step - 1],
                 axis, lax.rem(me + step, size))
        )
    for copy in again:
        copy.wait_recv()
    for copy in sent + again:
        copy.wait_send()


def total_over(values, axis, number):
    size = lax.axis_size(axis)
    dma = pltpu.SemaphoreType.DMA
    return pl.pallas_call(
        functools.partial(total_kernel, axis),
        out_shape=jax.ShapeDtypeStruct(values.shape, values.dtype),
        in_specs=[pl.BlockSpec(memory_space=pltpu.VMEM)],
        out_specs=pl.BlockSpec(memory_space=pltpu.VMEM),
        scratch_shapes=[pltpu.VMEM((size - 1,) + values.shape[1:], values.dtype)]
        + [dma((size - 1,))] * 4,
        compiler_params=pltpu.CompilerParams(
            collective_id=number, has_side_effects=True, vmem_limit_bytes=vmem_limit
        ),
        name="total_" + axis,
    )(values)


def local(
    tokens,
    attn_in_gain,
    query_weight,
    key_weight,
    value_weight,
    query_gain,
    key_gain,
    out_weight,
    attn_out_gain,
    ffn_in_gain,
    gate_weight,
    up_weight,
    down_weight,
    ffn_out_gain,
    cotangent,
):
    low = jnp.bfloat16
    size_b, size_c, size_h = (lax.axis_size(axis) for axis in ("batch", "ctx", "head"))
    ctx_index = lax.axis_index("ctx")
    head_index = lax.axis_index("head")
    tok, width = tokens.shape[1:]
    head_dim = key_gain.shape[0]
    n_q, n_k, n_o = query_weight.shape[1], key_weight.shape[1], out_weight.shape[0]
    shards = size_b * size_c
    heads = n_q * shards // head_dim
    scale = head_dim ** (-0.5)

    packed = jnp.concatenate([query_weight.T, key_weight.T, value_weight.T, out_weight], axis=0)
    full = gather(packed, "batch", "ctx", 0).reshape(shards, packed.shape[0], width)
    full_q = full[:, :n_q].reshape(-1, width)
    full_k = full[:, n_q : n_q + n_k].reshape(-1, width)
    full_v = full[:, n_q + n_k : n_q + 2 * n_k].reshape(-1, width)
    full_o = full[:, n_q + 2 * n_k :].reshape(-1, width)

    inputs = tokens[0].astype(jnp.float32)
    first_pos = (ctx_index * size_h + head_index) * tok
    query_pos = first_pos + jnp.arange(tok, dtype=jnp.int32)
    cosine, sine = angles(query_pos.astype(jnp.float32), head_dim)
    normed_f, pull_in = jax.vjp(rms_scale, inputs, attn_in_gain)
    normed_in = normed_f.astype(low)
    query_raw = contract_cols(normed_in, full_q).reshape(tok, heads, head_dim)
    key_raw = contract_cols(normed_in, full_k)
    value_low = contract_cols(normed_in, full_v).astype(low)

    def query_path(values, gain):
        return rotate(rms_scale(values, gain), cosine[:, None, :], sine[:, None, :])

    def key_path(values, gain):
        return rotate(rms_scale(values, gain), cosine, sine)

    query_rot, pull_query = jax.vjp(query_path, query_raw, query_gain)
    key_rot, pull_key = jax.vjp(key_path, key_raw, key_gain)
    key_low = key_rot.astype(low)
    rows = heads * tok
    query_rows = query_rot.astype(low).transpose(1, 0, 2).reshape(rows, head_dim)
    pairs = gather(jnp.concatenate([key_low, value_low], axis=1), "ctx", "head", 1)
    pairs = pairs.reshape(-1, 2 * head_dim)
    key_rows, value_rows = pairs[:, :head_dim], pairs[:, head_dim:]
    length = key_rows.shape[0]

    scores = contract_cols(query_rows, key_rows) * scale
    key_pos = jnp.arange(length, dtype=jnp.int32)
    row_pos = jnp.tile(query_pos, heads)
    scores = jnp.where(key_pos[None, :] <= row_pos[:, None], scores, -jnp.inf)
    row_max = jnp.max(scores, axis=1, keepdims=True)
    raised = jnp.exp(scores - row_max)
    probs = raised * (1.0 / jnp.sum(raised, axis=1, keepdims=True))
    probs_low = probs.astype(low)
    attended = jnp.dot(probs_low, value_rows, preferred_element_type=jnp.float32)

    def to_tokens(values):
        return values.reshape(heads, tok, head_dim).transpose(1, 0, 2).reshape(tok, -1)

    attended_tok = to_tokens(attended.astype(low))
    projected = jnp.dot(attended_tok, full_o, preferred_element_type=jnp.float32)
    post_attn, pull_aout = jax.vjp(rms_scale, projected, attn_out_gain)
    resid = inputs + post_attn
    normed_ffn_f, pull_fin = jax.vjp(rms_scale, resid, ffn_in_gain)
    group_ffn = gather(normed_ffn_f.astype(low), "batch", "ctx", 2).reshape(-1, width)
    gate_pre = jnp.dot(group_ffn, gate_weight, preferred_element_type=jnp.float32)
    up_pre = jnp.dot(group_ffn, up_weight, preferred_element_type=jnp.float32)
    hidden_f, pull_glu = jax.vjp(geglu, gate_pre, up_pre)
    hidden = hidden_f.astype(low)
    mixed_part = jnp.dot(hidden, down_weight, preferred_element_type=jnp.float32).astype(low)
    mixed = scatter_sum(mixed_part.reshape(size_b, size_c, tok, width), "batch", "ctx", 3)
    post_ffn, pull_fout = jax.vjp(rms_scale, mixed, ffn_out_gain)
    block_out = (resid + post_ffn).astype(low)

    out_grad = cotangent[0].astype(jnp.float32)
    mixed_grad_f, fout_gain_grad = pull_fout(out_grad)
    mixed_grad = gather(mixed_grad_f.astype(low), "batch", "ctx", 4).reshape(-1, width)
    hidden_grad = contract_cols(mixed_grad, down_weight)
    gate_grad_f, up_grad_f = pull_glu(hidden_grad)
    gate_grad = gate_grad_f.astype(low)
    up_grad = up_grad_f.astype(low)
    ffn_part = (contract_cols(gate_grad, gate_weight) + contract_cols(up_grad, up_weight)).astype(
        low
    )
    normed_ffn_grad = scatter_sum(ffn_part.reshape(size_b, size_c, tok, width), "batch", "ctx", 5)
    down_grad = contract_rows(hidden, mixed_grad).astype(low)
    gate_w_grad = contract_rows(gate_grad, group_ffn).astype(low)
    up_w_grad = contract_rows(up_grad, group_ffn).astype(low)
    resid_part, fin_gain_grad = pull_fin(normed_ffn_grad)
    resid_grad = out_grad + resid_part
    projected_grad_f, aout_gain_grad = pull_aout(resid_grad)
    projected_grad = projected_grad_f.astype(low)
    out_w_grad = contract_rows(attended_tok, projected_grad).astype(low)
    attended_grad = contract_cols(projected_grad, full_o).astype(low)
    grad_rows = attended_grad.reshape(tok, heads, head_dim).transpose(1, 0, 2).reshape(rows, head_dim)
    delta = jnp.sum(grad_rows.astype(jnp.float32) * attended, axis=1)

    probs_grad = contract_cols(grad_rows, value_rows)
    score_grad = (probs * (probs_grad - delta[:, None])).astype(low)
    query_low_grad = jnp.dot(score_grad, key_rows, preferred_element_type=jnp.float32) * scale
    key_part = contract_rows(score_grad, query_rows) * scale
    value_part = contract_rows(probs_low, grad_rows)
    pair_part = jnp.concatenate([key_part.astype(low), value_part.astype(low)], axis=1)
    pair_grad = scatter_sum(
        pair_part.reshape(size_c, size_h, tok, 2 * head_dim), "ctx", "head", 6
    )
    key_low_grad, value_grad = pair_grad[:, :head_dim], pair_grad[:, head_dim:].astype(low)
    query_low_grad = to_tokens(query_low_grad.astype(low)).reshape(tok, heads, head_dim)
    query_raw_grad_f, query_gain_grad = pull_query(query_low_grad.astype(jnp.float32))
    key_raw_grad_f, key_gain_grad = pull_key(key_low_grad)
    query_raw_grad = query_raw_grad_f.reshape(tok, heads * head_dim).astype(low)
    key_raw_grad = key_raw_grad_f.astype(low)
    query_w_grad = contract_rows(query_raw_grad, normed_in).astype(low)
    key_w_grad = contract_rows(key_raw_grad, normed_in).astype(low)
    value_w_grad = contract_rows(value_grad, normed_in).astype(low)
    normed_in_grad = (
        jnp.dot(query_raw_grad, full_q, preferred_element_type=jnp.float32)
        + jnp.dot(key_raw_grad, full_k, preferred_element_type=jnp.float32)
        + jnp.dot(value_grad, full_v, preferred_element_type=jnp.float32)
    )
    inputs_part, ain_gain_grad = pull_in(normed_in_grad)
    inputs_grad = resid_grad + inputs_part

    gains = (
        ain_gain_grad,
        query_gain_grad,
        key_gain_grad,
        aout_gain_grad,
        fin_gain_grad,
        fout_gain_grad,
    )
    gain_flat = jnp.concatenate(gains)
    gain_rows = -(-gain_flat.shape[0] // width)
    gain_pad = -(-gain_rows // 16) * 16
    gain_block = jnp.pad(gain_flat, (0, gain_pad * width - gain_flat.shape[0])).astype(low)
    gain_block = jnp.broadcast_to(gain_block.reshape(1, gain_pad, width), (shards, gain_pad, width))
    split = (
        query_w_grad.reshape(shards, n_q, width),
        key_w_grad.reshape(shards, n_k, width),
        value_w_grad.reshape(shards, n_k, width),
        out_w_grad.reshape(shards, n_o, width),
        gain_block,
    )
    grads = jnp.concatenate(split, axis=1)
    depth = grads.shape[1]
    summed = scatter_sum(
        grads.reshape(size_b, size_c, depth, width), "batch", "ctx", 7, low
    )
    stacked = jnp.concatenate([summed, gate_w_grad, up_w_grad, down_grad], axis=0)
    unit = 16 * size_h
    used = stacked.shape[0]
    stacked = jnp.pad(stacked, ((0, -used % unit), (0, 0)))
    done = total_over(stacked.reshape(size_h, -1, width), "head", 8)
    done = done.reshape(-1, width).astype(jnp.float32)

    parts = []
    start = 0
    n_f = gate_weight.shape[1]
    for count in (n_q, n_k, n_k, n_o, gain_pad, n_f, n_f, n_f):
        parts.append(done[start : start + count])
        start += count
    gain_done = parts[4].reshape(-1)
    gain_out = []
    start = 0
    for gain in gains:
        gain_out.append(gain_done[start : start + gain.shape[0]])
        start += gain.shape[0]
    return (
        block_out[None],
        inputs_grad[None],
        gain_out[0],
        parts[0].T,
        parts[1].T,
        parts[2].T,
        gain_out[1],
        gain_out[2],
        parts[3],
        gain_out[3],
        gain_out[4],
        parts[5].T,
        parts[6].T,
        parts[7],
        gain_out[5],
    )


def solution(mesh):
    in_specs = (
        P("batch", ("ctx", "head"), None),
        P(),
        P(None, ("batch", "ctx")),
        P(None, ("batch", "ctx")),
        P(None, ("batch", "ctx")),
        P(),
        P(),
        P(("batch", "ctx"), None),
        P(),
        P(),
        P(None, ("batch", "ctx")),
        P(None, ("batch", "ctx")),
        P(("batch", "ctx"), None),
        P(),
        P("batch", ("ctx", "head"), None),
    )
    out_specs = (
        P("batch", ("ctx", "head"), None),
        P("batch", ("ctx", "head"), None),
        P(),
        P(None, ("batch", "ctx")),
        P(None, ("batch", "ctx")),
        P(None, ("batch", "ctx")),
        P(),
        P(),
        P(("batch", "ctx"), None),
        P(),
        P(),
        P(None, ("batch", "ctx")),
        P(None, ("batch", "ctx")),
        P(("batch", "ctx"), None),
        P(),
    )
    return jax.shard_map(local, mesh=mesh, in_specs=in_specs, out_specs=out_specs, check_vma=False)
```

time: 1060 us -> 325 us (0.31)
  waiting for transfers between devices: 810 us -> 0 us
  Pallas kernels: 0 us -> 269 us
  blocking collectives: 126 us -> 0 us
  other arithmetic: 33.8 us -> 11.3 us
  starting transfers between devices: 21.7 us -> 0 us
  matrix products: 38.4 us -> 20.5 us
  between operations: 14.9 us -> 1.87 us
    reduce_scatter x9 -> x0, waiting for transfers between devices: 626 us -> none  [the longest x1 105 us: local(): lax.psum_scatter(weight_grads[4], ('batch', 'ctx'), scatter_dimension=1,...]
    pallas_call x0 -> x9, Pallas kernels: none -> 269 us  [the longest x4 120 us: scatter_sum(): pl.pallas_call(functools.partial(scatter_kernel, first, second), out_shap...]
    all_gather x5 -> x0, waiting for transfers between devices: 143 us -> none  [the longest x1 53.7 us: local(): lax.all_gather(up_weight, ('batch', 'ctx'), axis=1, tiled=True)]
    all_gather x4 -> x0, blocking collectives: 70.6 us -> none  [the longest x1 25.6 us: local(): lax.all_gather(value_weight, ('batch', 'ctx'), axis=1, tiled=True)]
    psum x1 -> x0, blocking collectives: 39.5 us -> none  [local(): lax.psum((ain_gain_grad, query_gain_grad, key_gain_grad, aout_gain_grad,...]
    psum x2 -> x0, waiting for transfers between devices: 32.3 us -> none  [the longest x1 32.3 us: local(): lax.psum(shards[0].astype(jnp.bfloat16), 'head').astype(jnp.float32)]
    all_to_all x2 -> x0, starting transfers between devices: 21.1 us -> none  [the longest x1 15.9 us: local(): lax.all_to_all(query_low, 'head', split_axis=1, concat_axis=0, tiled=True)]
    convert_element_type x20 -> x7, other arithmetic: 24 us -> 3.07 us  [the longest x1 0.91 us: local(): query_raw_grad = query_raw_grad_f.reshape(tok, heads * head_dim).astype(low)]
  transfers between devices with their start and end apart: 18 -> 0, of which waited for: 14 -> 0; matrix products, arithmetic and copies ran while one was open for 5% -> 0% of each run, Pallas kernels for 0% -> 0%
where the time goes in v1:
time: 325 us; the launch traced here: 324 us
  Pallas kernels  269 us (83%)
  local copies, waits for them, and re-layouts  21.7 us (7%)
  matrix products  20.5 us (6%)
  other arithmetic  11.3 us (3%)
    pallas_call x4, Pallas kernels, scatter_sum(): pl.pallas_call(functools.partial(scatter_kernel, first, second), out_shap...  120 us
    pallas_call x4, Pallas kernels, gather(): pl.pallas_call(functools.partial(gather_kernel, first, second), out_shape...  113 us
    pallas_call x1, Pallas kernels, total_over(): pl.pallas_call(functools.partial(total_kernel, axis), out_shape=jax.Shape...  35.8 us
    unnamed x119, local copies, waits for them, and re-layouts  11.3 us
    dot_general x9, matrix products, contract_rows(): lax.dot_general(left, right, (((0,), (0,)), ((), ())), preferred_element_...  7.96 us

profile of v1, /device:TPU:9, one launch (start us, length us, event | category | flops | bytes accessed | tf_op | source)
XLA Modules:
  0.0 324.0 jit_solution(13773808978418599669)
XLA Ops:
  0.7 1.1 fusion.36
  1.8 0.4 copy-done.50
  2.3 1.1 copy.36
  3.3 1.0 pad_maximum_fusion.1.x_ref
  4.3 50.1 %gather_batch_ctx.3 = bf16[4,2,320,640]{3,2,1,0:T(8,128)(2,1)} custom-call(bf16[320,640]{1,0:T(8,128)(2,1)S(1)} %pad_maximum_fusion.1.x_ref), custom_call_target="tpu_custom_call" | custom-call | tf_op jit(solution)/shard_map/gather_batch_ctx/pallas_call | solution.py:120
  54.4 1.1 fusion.83
  55.6 2.3 fusion.82
  58.2 0.3 multiply_reduce_fusion.13
  58.7 0.3 multiply_cosine_fusion
  59.1 0.6 multiply_reduce_fusion.3
  60.1 0.5 copy-done.4
  60.6 14.7 %gather_ctx_head.1 = bf16[2,4,128,512]{3,2,1,0:T(8,128)(2,1)S(1)} custom-call(bf16[128,512]{1,0:T(8,128)(2,1)S(1)} %pad_maximum_fusion.3.x_ref), custom_call_target="tpu_custom_call" | custom-call | tf_op jit(solution)/shard_map/gather_ctx_head/pallas_call | solution.py:120
  75.3 0.6 fusion.4
  75.9 0.7 fusion.80
  76.7 1.6 fusion.88
  78.5 0.5 multiply_reduce_fusion.10
  79.4 29.8 %gather_batch_ctx.4 = bf16[4,2,128,640]{3,2,1,0:T(8,128)(2,1)S(1)} custom-call(bf16[128,640]{1,0:T(8,128)(2,1)S(1)} %multiply_convert_fusion.4.x_ref), custom_call_target="tpu_custom_call" | custom-call | tf_op jit(solution)/shard_map/gather_batch_ctx/pallas_call | solution.py:120
  109.1 0.6 fusion.89
  109.7 0.6 multiply_convert_fusion.3
  110.4 0.6 convolution_convert_fusion
  111.0 27.1 %scatter_batch_ctx.3 = f32[128,640]{1,0:T(8,128)S(1)} custom-call(bf16[4,2,128,640]{3,2,1,0:T(8,128)(2,1)S(1)} %bitcast.158), custom_call_target="tpu_custom_call" | custom-call | tf_op jit(solution)/shard_map/scatter_batch_ctx/pallas_call | solution.py:180
  138.4 0.8 fusion.40
  139.3 18.4 %gather_batch_ctx.5 = bf16[4,2,128,640]{3,2,1,0:T(8,128)(2,1)S(1)} custom-call(bf16[128,640]{1,0:T(8,128)(2,1)S(1)} %get-tuple-element.77.x_ref), custom_call_target="tpu_custom_call" | custom-call | tf_op jit(solution)/shard_map/gather_batch_ctx/pallas_call | solution.py:120
  157.7 1.2 multiply_convert_fusion.2
  158.9 1.3 convolution_convert_fusion.4
  160.2 1.3 convolution_convert_fusion.5
  161.5 1.3 convolution_convert_fusion.6
  162.8 0.6 fusion.90
  163.4 0.6 add_convert_fusion
  164.0 19.6 %scatter_batch_ctx.4 = f32[128,640]{1,0:T(8,128)S(1)} custom-call(bf16[4,2,128,640]{3,2,1,0:T(8,128)(2,1)S(1)} %bitcast.153), custom_call_target="tpu_custom_call" | custom-call | tf_op jit(solution)/shard_map/scatter_batch_ctx/pallas_call | solution.py:180
  184.2 0.5 convolution_convert_fusion.9
  185.0 0.8 copy-done.12
  185.7 0.9 convolution_convert_fusion.3
  186.7 0.8 multiply_convert_fusion
  187.5 1.1 fusion.9
  188.7 0.5 fusion.8
  189.3 0.5 copy.40
  189.9 19.4 %scatter_ctx_head.1 = f32[128,512]{1,0:T(8,128)S(1)} custom-call(bf16[2,4,128,512]{3,2,1,0:T(8,128)(2,1)S(1)} %bitcast.159), custom_call_target="tpu_custom_call" | custom-call | tf_op jit(solution)/shard_map/scatter_ctx_head/pallas_call | solution.py:180
  209.3 0.3 fusion.65
  209.8 0.7 multiply_multiply_fusion.7
  210.5 0.7 fusion.52
  211.7 0.9 fusion.17
  212.6 1.1 copy.39
  213.7 0.4 fusion.91
  214.4 1.3 fusion.35
  216.8 0.4 dynamic-update-slice.10
  217.2 0.9 fusion.43
  218.1 0.3 convolution_convert_fusion.7
  218.8 0.5 convolution_convert_fusion.1
  219.3 1.5 convolution_convert_fusion.2
  221.3 1.7 copy-done.6
  223.0 53.7 %scatter_batch_ctx.5 = bf16[336,640]{1,0:T(8,128)(2,1)S(1)} custom-call(bf16[4,2,336,640]{3,2,1,0:T(8,128)(2,1)} %copy-done.6), custom_call_target="tpu_custom_call" | custom-call | tf_op jit(solution)/shard_map/scatter_batch_ctx/pallas_call | solution.py:180
  276.8 1.2 fusion.7
  278.0 35.8 %total_head.1 = bf16[4,288,640]{2,1,0:T(8,128)(2,1)S(1)} custom-call(bf16[4,288,640]{2,1,0:T(8,128)(2,1)} %bitcast.172), custom_call_target="tpu_custom_call" | custom-call | tf_op jit(solution)/shard_map/total_head/pallas_call | solution.py:232
  313.8 0.3 bitcast_convert_fusion
  314.2 0.6 slice_reduce_fusion
  314.8 0.6 fusion.87
  315.4 0.6 fusion.86
  316.0 0.7 slice_bitcast_fusion.3
  316.6 0.9 fusion.85
  317.5 1.3 fusion.84
  318.8 1.9 copy.41
  320.8 2.2 copy.43
  322.9 1.1 copy.42
  (155 shorter events, 5.1 us)
Async XLA Ops:
  0.6 109.8 %copy-start = (bf16[256,640]{1,0:T(8,128)(2,1)S(1)}, bf16[256,640]{1,0:T(8,128)(2,1)}, u32[]{:S(2)}) copy-start(bf16[256,640]{1,0:T(8,128)(2,1)} %param.27) | copy-start | bytes 983044
  1.7 0.5 copy-start.50
  1.8 56.9 %copy-start.44 = (f32[128]{0:T(128)}, f32[128]{0:T(128)S(1)}, u32[]{:S(2)}) copy-start(f32[128]{0:T(128)S(1)} %multiply_exponential_fusion) | copy-start | bytes 1540
  1.8 56.9 %copy-start.46 = (f32[128]{0:T(128)}, f32[128]{0:T(128)S(1)}, u32[]{:S(2)}) copy-start(f32[128]{0:T(128)S(1)} %get-tuple-element.106) | copy-start | bytes 1540
  55.5 2.7 copy-start.16
  55.5 3.5 %copy-start.18 = (bf16[8,32,640]{2,1,0:T(8,128)(2,1)}, bf16[8,32,640]{2,1,0:T(8,128)(2,1)S(1)}, u32[]{:S(2)}) copy-start(bf16[8,32,640]{2,1,0:T(8,128)(2,1)S(1)} %get-tuple-element.63) | copy-start | bytes 983044
  55.5 2.4 copy-start.3
  55.5 2.4 copy-start.33
  55.6 3.0 copy-start.37
  57.9 2.0 copy-start.1
  57.9 1.9 copy-start.38
  58.5 0.5 copy-start.52
  58.6 1.5 copy-start.20
  58.6 1.4 copy-start.40
  59.0 1.0 copy-start.22
  59.8 0.8 copy-start.4
  60.5 15.3 %copy-start.31 = (bf16[128,4,256]{2,0,1:T(8,128)(2,1)}, bf16[128,4,256]{2,0,1:T(8,128)(2,1)S(1)}, u32[]{:S(2)}) copy-start(bf16[128,4,256]{2,0,1:T(8,128)(2,1)S(1)} %pad_maximum_fusion.2) | copy-start | bytes 786436
  75.9 0.8 copy-start.42
  75.9 2.4 copy-start.11
  76.7 1.6 copy-start.48
  78.3 0.7 copy-start.34
  78.3 0.9 copy-start.35
  78.5 30.6 %copy-start.8 = (bf16[4,128,256]{1,2,0:T(8,128)(2,1)}, bf16[4,128,256]{1,2,0:T(8,128)(2,1)S(1)}, u32[]{:S(2)}) copy-start(bf16[4,128,256]{1,2,0:T(8,128)(2,1)S(1)} %copy.37) | copy-start | bytes 786436
  78.5 30.6 %copy-start.19 = (bf16[640,256]{1,0:T(8,128)(2,1)S(1)}, bf16[640,256]{1,0:T(8,128)(2,1)}, u32[]{:S(2)}) copy-start(bf16[640,256]{1,0:T(8,128)(2,1)} %param.25) | copy-start | bytes 983044
  79.3 30.4 %copy-start.26 = (bf16[640,256]{1,0:T(8,128)(2,1)S(1)}, bf16[640,256]{1,0:T(8,128)(2,1)}, u32[]{:S(2)}) copy-start(bf16[640,256]{1,0:T(8,128)(2,1)} %param.26) | copy-start | bytes 983044
  110.4 27.9 %copy-start.13 = (bf16[1,128,640]{2,1,0:T(8,128)(2,1)S(1)}, bf16[1,128,640]{2,1,0:T(8,128)(2,1)}, u32[]{:S(2)}) copy-start(bf16[1,128,640]{2,1,0:T(8,128)(2,1)} %param.29) | copy-start | bytes 491524
  110.4 27.9 %copy-start.36 = (f32[640]{0:T(1024)S(1)}, f32[640]{0:T(1024)}, u32[]{:S(2)}) copy-start(f32[640]{0:T(1024)} %param.28) | copy-start | bytes 7684
  183.7 1.1 copy-start.25
  184.0 1.7 copy-start.12
  184.0 1.7 copy-start.43
  184.1 1.7 copy-start.49
  184.2 2.5 copy-start.14
  187.5 1.2 copy-start.32
  189.3 20.0 %copy-start.45 = (f32[128]{0:T(128)S(1)}, f32[128]{0:T(128)}, u32[]{:S(2)}) copy-start(f32[128]{0:T(128)} %copy-done.44) | copy-start | bytes 1540
  189.3 20.0 %copy-start.47 = (f32[128]{0:T(128)S(1)}, f32[128]{0:T(128)}, u32[]{:S(2)}) copy-start(f32[128]{0:T(128)} %copy-done.46) | copy-start | bytes 1540
  189.3 20.4 %copy-start.21 = (f32[128,256]{1,0:T(8,128)S(1)}, f32[128,256]{1,0:T(8,128)}, u32[]{:S(2)}) copy-start(f32[128,256]{1,0:T(8,128)} %copy-done.20) | copy-start | bytes 393220
  189.3 20.4 %copy-start.41 = (f32[128]{0:T(128)S(1)}, f32[128]{0:T(128)}, u32[]{:S(2)}) copy-start(f32[128]{0:T(128)} %copy-done.40) | copy-start | bytes 1540
  189.3 21.9 %copy-start.30 = (bf16[512,256]{1,0:T(8,128)(2,1)S(1)}, bf16[512,256]{1,0:T(8,128)(2,1)}, u32[]{:S(2)}) copy-start(bf16[512,256]{1,0:T(8,128)(2,1)} %fusion.9) | copy-start | bytes 786436
  189.9 21.4 %copy-start.23 = (f32[128,128]{1,0:T(8,128)S(1)}, f32[128,128]{1,0:T(8,128)}, u32[]{:S(2)}) copy-start(f32[128,128]{1,0:T(8,128)} %copy-done.22) | copy-start | bytes 196612
  189.9 21.5 %copy-start.5 = (f32[128,4,256]{2,0,1:T(8,128)S(1)}, f32[128,4,256]{2,0,1:T(8,128)}, u32[]{:S(2)}) copy-start(f32[128,4,256]{2,0,1:T(8,128)} %copy-done.4) | copy-start | bytes 1572868
  211.3 2.4 copy-start.2
  211.6 2.5 copy-start.17
  211.6 2.5 copy-start.24
  213.7 5.1 %copy-start.10 = (bf16[128,4,256]{0,2,1:T(8,128)(2,1)}, bf16[128,4,256]{0,2,1:T(8,128)(2,1)S(1)}, u32[]{:S(2)}) copy-start(bf16[128,4,256]{0,2,1:T(8,128)(2,1)S(1)} %copy.39) | copy-start | bytes 786436
  213.7 2.0 copy-start.39
  213.7 3.5 %copy-start.51 = (f32[128]{0:T(128)S(1)}, f32[128]{0:T(128)}, u32[]{:S(2)}) copy-start(f32[128]{0:T(128)} %copy-done.50) | copy-start | bytes 1540
  214.4 4.4 %copy-start.9 = (bf16[4,128,256]{1,2,0:T(8,128)(2,1)S(1)}, bf16[4,128,256]{1,2,0:T(8,128)(2,1)}, u32[]{:S(2)}) copy-start(bf16[4,128,256]{1,2,0:T(8,128)(2,1)} %copy-done.8) | copy-start | bytes 786436
  214.4 4.4 %copy-start.15 = (bf16[128,640]{1,0:T(8,128)(2,1)S(1)}, bf16[128,640]{1,0:T(8,128)(2,1)}, u32[]{:S(2)}) copy-start(bf16[128,640]{1,0:T(8,128)(2,1)} %copy-done.14) | copy-start | bytes 491524
  221.2 55.5 %copy-start.27 = (bf16[256,640]{1,0:T(8,128)(2,1)S(1)}, bf16[256,640]{1,0:T(8,128)(2,1)}, u32[]{:S(2)}) copy-start(bf16[256,640]{1,0:T(8,128)(2,1)} %convolution_convert_fusion.4) | copy-start | bytes 983044
  221.3 55.5 %copy-start.28 = (bf16[256,640]{1,0:T(8,128)(2,1)S(1)}, bf16[256,640]{1,0:T(8,128)(2,1)}, u32[]{:S(2)}) copy-start(bf16[256,640]{1,0:T(8,128)(2,1)} %convolution_convert_fusion.5) | copy-start | bytes 983044
  221.3 55.5 %copy-start.29 = (bf16[256,640]{1,0:T(8,128)(2,1)S(1)}, bf16[256,640]{1,0:T(8,128)(2,1)}, u32[]{:S(2)}) copy-start(bf16[256,640]{1,0:T(8,128)(2,1)} %convolution_convert_fusion.6) | copy-start | bytes 983044
  221.3 1.7 copy-start.6
  318.8 4.1 %copy-start.7 = (f32[640,256]{0,1:T(8,128)S(1)}, f32[640,256]{0,1:T(8,128)}, u32[]{:S(2)}) copy-start(f32[640,256]{0,1:T(8,128)} %get-tuple-element.66) | copy-start | bytes 1966084

commit v2 on v1

--- a/solution.py
+++ b/solution.py
@@ -198,49 +198,271 @@
     )(values)
 
 
-def total_kernel(axis, x_ref, out_ref, held, send_a, recv_a, send_b, recv_b):
-    size = lax.axis_size(axis)
-    me = lax.axis_index(axis)
-    greet((axis,))
-    sent = []
-    for step in range(1, size):
-        other = lax.rem(me + step, size)
-        sent.append(
-            send(x_ref.at[other], held.at[step - 1], send_a.at[step - 1], recv_a.at[step - 1],
-                 axis, other)
-        )
-    total = x_ref[me].astype(jnp.float32)
-    for step in range(1, size):
-        sent[step - 1].wait_recv()
-        total += held[step - 1].astype(jnp.float32)
-    out_ref[me] = total.astype(out_ref.dtype)
-    again = []
-    for step in range(1, size):
-        again.append(
-            send(out_ref.at[me], out_ref.at[me], send_b.at[step - 1], recv_b.at[step - 1],
-                 axis, lax.rem(me + step, size))
-        )
-    for copy in again:
+def greet_all(axes, head_steps):
+    barrier = pltpu.get_barrier_semaphore()
+    peers = []
+    for axis in axes:
+        size = lax.axis_size(axis)
+        peers += [(axis, lax.rem(lax.axis_index(axis) + step, size)) for step in range(1, size)]
+    peers += [("head", index) for index in head_steps]
+    for axis, index in peers:
+        pl.semaphore_signal(
+            barrier, inc=1, device_id={axis: index}, device_id_type=pl.DeviceIdType.MESH
+        )
+    pl.semaphore_wait(barrier, len(peers))
+
+
+def head_place():
+    size = lax.axis_size("head")
+    at_h = lax.axis_index("head")
+    low_bit = lax.rem(at_h, 2)
+    partner = at_h + 1 - 2 * low_bit
+    likes = [lax.rem(at_h + 2 * step, size) for step in range(1, size // 2)]
+    return at_h, low_bit, partner, likes
+
+
+def weights_kernel(
+    x_ref, out_ref, own_sem, send_a, recv_a, send_b, recv_b, send_h, recv_h, send_l, recv_l
+):
+    size_a, size_b, size_h = (lax.axis_size(axis) for axis in ("batch", "ctx", "head"))
+    at_a, at_b = lax.axis_index("batch"), lax.axis_index("ctx")
+    at_h, low_bit, partner, likes = head_place()
+    greet_all(("batch", "ctx"), likes + [partner])
+    own = out_ref.at[at_a, at_b, at_h]
+    sent_a, sent_b, sent_h, sent_l = {}, {}, {}, {}
+    for step in range(1, size_a):
+        sent_a[step] = send(
+            x_ref.at[at_h], own, send_a.at[step - 1], recv_a.at[step - 1], "batch",
+            lax.rem(at_a + step, size_a),
+        )
+
+    def to_ctx(source, target, step):
+        for turn in range(1, size_b):
+            sent_b[step, turn] = send(
+                source, target, send_b.at[step, turn - 1], recv_b.at[step, turn - 1], "ctx",
+                lax.rem(at_b + turn, size_b),
+            )
+
+    to_ctx(x_ref.at[at_h], own, 0)
+    keep = pltpu.make_async_copy(x_ref, out_ref.at[at_a, at_b], own_sem)
+    keep.start()
+
+    def slot(step, turn, head):
+        return out_ref.at[
+            lax.rem(at_a + size_a - step, size_a), lax.rem(at_b + size_b - turn, size_b), head
+        ]
+
+    def to_head(step, turn):
+        here = slot(step, turn, at_h)
+        for jump, like in enumerate(likes):
+            sent_h[step, turn, jump] = send(
+                here, here, send_h.at[step, turn, jump], recv_h.at[step, turn, jump], "head", like
+            )
+        sent_l[step, turn, 0] = send(
+            here, here, send_l.at[step, turn, 0], recv_l.at[step, turn, 0], "head", partner
+        )
+
+    for step in range(1, size_a):
+        sent_a[step].wait_recv()
+        here = slot(step, 0, at_h)
+        to_ctx(here, here, step)
+        to_head(step, 0)
+    for step in range(size_a):
+        for turn in range(1, size_b):
+            sent_b[step, turn].wait_recv()
+            to_head(step, turn)
+    for step, turn, jump in list(sent_h):
+        sent_h[step, turn, jump].wait_recv()
+        back = lax.rem(at_h + size_h - 2 * (jump + 1), size_h)
+        here = slot(step, turn, back)
+        sent_l[step, turn, jump + 1] = send(
+            here, here, send_l.at[step, turn, jump + 1], recv_l.at[step, turn, jump + 1],
+            "head", partner,
+        )
+    for copy in sent_l.values():
         copy.wait_recv()
-    for copy in sent + again:
-        copy.wait_send()
-
-
-def total_over(values, axis, number):
-    size = lax.axis_size(axis)
+    for sent in (sent_a, sent_b, sent_h, sent_l):
+        for copy in sent.values():
+            copy.wait_send()
+    keep.wait()
+
+
+def gather_weights(values, number):
+    size_a, size_b, size_h = (lax.axis_size(axis) for axis in ("batch", "ctx", "head"))
     dma = pltpu.SemaphoreType.DMA
+    pairs = size_h // 2
     return pl.pallas_call(
-        functools.partial(total_kernel, axis),
-        out_shape=jax.ShapeDtypeStruct(values.shape, values.dtype),
-        in_specs=[pl.BlockSpec(memory_space=pltpu.VMEM)],
-        out_specs=pl.BlockSpec(memory_space=pltpu.VMEM),
-        scratch_shapes=[pltpu.VMEM((size - 1,) + values.shape[1:], values.dtype)]
-        + [dma((size - 1,))] * 4,
+        weights_kernel,
+        out_shape=jax.ShapeDtypeStruct((size_a, size_b) + values.shape, values.dtype),
+        in_specs=[pl.BlockSpec(memory_space=pl.ANY)],
+        out_specs=pl.BlockSpec(memory_space=pl.ANY),
+        scratch_shapes=[dma]
+        + [dma((size_a - 1,))] * 2
+        + [dma((size_a, size_b - 1))] * 2
+        + [dma((size_a, size_b, pairs - 1))] * 2
+        + [dma((size_a, size_b, pairs))] * 2,
         compiler_params=pltpu.CompilerParams(
             collective_id=number, has_side_effects=True, vmem_limit_bytes=vmem_limit
         ),
-        name="total_" + axis,
+        name="gather_weights",
     )(values)
+
+
+def grads_kernel(
+    x_ref, w_ref, out_ref, wout_ref,
+    r_low, p_ctx, r_ctx, p_batch, r_batch, p_like, r_like, w_low, wp_like, w_like,
+    send_low, recv_low, send_c, recv_c, send_b, recv_b, send_k, recv_k, send_o, recv_o,
+    wsend_low, wrecv_low, wsend_k, wrecv_k, wsend_h, wrecv_h, wsend_o, wrecv_o,
+):
+    f32 = jnp.float32
+    size_a, size_b, size_h = (lax.axis_size(axis) for axis in ("batch", "ctx", "head"))
+    at_a, at_b = lax.axis_index("batch"), lax.axis_index("ctx")
+    at_h, low_bit, partner, likes = head_place()
+    pairs = size_h // 2
+    other = 1 - low_bit
+    greet_all(("batch", "ctx"), likes + [partner])
+    order = list(range(1, size_a)) + [0]
+    turns = list(range(1, size_b)) + [0]
+
+    def goal(step, turn):
+        return lax.rem(at_a + step, size_a), lax.rem(at_b + turn, size_b)
+
+    low_sent, ctx_sent, batch_sent, like_sent = {}, {}, {}, {}
+    w_low_sent, w_like_sent, w_all, w_out = {}, {}, {}, {}
+    for turn in turns:
+        for step in order:
+            goal_a, goal_b = goal(step, turn)
+            low_sent[step, turn] = send(
+                x_ref.at[goal_a, goal_b, other], r_low.at[step, turn],
+                send_low.at[step, turn], recv_low.at[step, turn], "head", partner,
+            )
+    for jump in list(range(1, pairs)) + [0]:
+        theirs = lax.rem(partner + 2 * jump, size_h)
+        w_low_sent[jump] = send(
+            w_ref.at[theirs], w_low.at[jump], wsend_low.at[jump], wrecv_low.at[jump],
+            "head", partner,
+        )
+
+    def pair_sum(step, turn):
+        goal_a, goal_b = goal(step, turn)
+        low_sent[step, turn].wait_recv()
+        return x_ref[goal_a, goal_b, low_bit].astype(f32) + r_low[step, turn].astype(f32)
+
+    for turn in range(1, size_b):
+        for step in order:
+            p_ctx[step, turn - 1] = pair_sum(step, turn).astype(p_ctx.dtype)
+            ctx_sent[step, turn] = send(
+                p_ctx.at[step, turn - 1], r_ctx.at[step, turn - 1],
+                send_c.at[step, turn - 1], recv_c.at[step, turn - 1], "ctx", goal(step, turn)[1],
+            )
+    for jump in range(1, pairs):
+        w_low_sent[jump].wait_recv()
+        like = likes[jump - 1]
+        wp_like[jump - 1] = (w_ref[like].astype(f32) + w_low[jump].astype(f32)).astype(
+            wp_like.dtype
+        )
+        w_like_sent[jump] = send(
+            wp_like.at[jump - 1], w_like.at[jump - 1],
+            wsend_k.at[jump - 1], wrecv_k.at[jump - 1], "head", like,
+        )
+
+    def ctx_sum(step):
+        total = pair_sum(step, 0)
+        for turn in range(1, size_b):
+            ctx_sent[step, turn].wait_recv()
+            total += r_ctx[step, turn - 1].astype(f32)
+        return total
+
+    for step in range(1, size_a):
+        p_batch[step - 1] = ctx_sum(step).astype(p_batch.dtype)
+        batch_sent[step] = send(
+            p_batch.at[step - 1], r_batch.at[step - 1],
+            send_b.at[step - 1], recv_b.at[step - 1], "batch", goal(step, 0)[0],
+        )
+    total = ctx_sum(0)
+    w_low_sent[0].wait_recv()
+    w_total = w_ref[at_h].astype(f32) + w_low[0].astype(f32)
+    for jump in range(1, pairs):
+        w_like_sent[jump].wait_recv()
+        w_total += w_like[jump - 1].astype(f32)
+    wout_ref[at_h] = w_total.astype(wout_ref.dtype)
+    w_own = wout_ref.at[at_h]
+    for jump in range(1, pairs):
+        w_all[jump] = send(
+            w_own, w_own, wsend_h.at[jump - 1], wrecv_h.at[jump - 1], "head", likes[jump - 1]
+        )
+    w_out[0] = send(w_own, w_own, wsend_o.at[0], wrecv_o.at[0], "head", partner)
+
+    for step in range(1, size_a):
+        batch_sent[step].wait_recv()
+        total += r_batch[step - 1].astype(f32)
+    p_like[...] = total.astype(p_like.dtype)
+    for jump in range(1, pairs):
+        like_sent[jump] = send(
+            p_like, r_like.at[jump - 1], send_k.at[jump - 1], recv_k.at[jump - 1],
+            "head", likes[jump - 1],
+        )
+    for jump in range(1, pairs):
+        w_all[jump].wait_recv()
+        slot = wout_ref.at[lax.rem(at_h + size_h - 2 * jump, size_h)]
+        w_out[jump] = send(slot, slot, wsend_o.at[jump], wrecv_o.at[jump], "head", partner)
+    total = p_like[...].astype(f32)
+    for jump in range(1, pairs):
+        like_sent[jump].wait_recv()
+        total += r_like[jump - 1].astype(f32)
+    out_ref[low_bit] = total.astype(out_ref.dtype)
+    last = send(out_ref.at[low_bit], out_ref.at[low_bit], send_o, recv_o, "head", partner)
+    for copy in w_out.values():
+        copy.wait_recv()
+    last.wait_recv()
+    last.wait_send()
+    for sent in (
+        low_sent, ctx_sent, batch_sent, like_sent, w_low_sent, w_like_sent, w_all, w_out
+    ):
+        for copy in sent.values():
+            copy.wait_send()
+
+
+def sum_grads(values, wide, number):
+    size_a, size_b, size_h = (lax.axis_size(axis) for axis in ("batch", "ctx", "head"))
+    pairs = size_h // 2
+    block, wide_block = values.shape[3:], wide.shape[1:]
+    kind = values.dtype
+    dma = pltpu.SemaphoreType.DMA
+    vmem = pl.BlockSpec(memory_space=pltpu.VMEM)
+    return pl.pallas_call(
+        grads_kernel,
+        out_shape=(
+            jax.ShapeDtypeStruct((2,) + block, kind),
+            jax.ShapeDtypeStruct(wide.shape, kind),
+        ),
+        in_specs=[vmem, vmem],
+        out_specs=(vmem, vmem),
+        scratch_shapes=[
+            pltpu.VMEM((size_a, size_b) + block, kind),
+            pltpu.VMEM((size_a, size_b - 1) + block, kind),
+            pltpu.VMEM((size_a, size_b - 1) + block, kind),
+            pltpu.VMEM((size_a - 1,) + block, kind),
+            pltpu.VMEM((size_a - 1,) + block, kind),
+            pltpu.VMEM(block, kind),
+            pltpu.VMEM((pairs - 1,) + block, kind),
+            pltpu.VMEM((pairs,) + wide_block, kind),
+            pltpu.VMEM((pairs - 1,) + wide_block, kind),
+            pltpu.VMEM((pairs - 1,) + wide_block, kind),
+        ]
+        + [dma((size_a, size_b))] * 2
+        + [dma((size_a, size_b - 1))] * 2
+        + [dma((size_a - 1,))] * 2
+        + [dma((pairs - 1,))] * 2
+        + [dma] * 2
+        + [dma((pairs,))] * 2
+        + [dma((pairs - 1,))] * 4
+        + [dma((pairs,))] * 2,
+        compiler_params=pltpu.CompilerParams(
+            collective_id=number, has_side_effects=True, vmem_limit_bytes=vmem_limit
+        ),
+        name="sum_grads",
+    )(values, wide)
 
 
 def local(
@@ -272,11 +494,12 @@
     scale = head_dim ** (-0.5)
 
     packed = jnp.concatenate([query_weight.T, key_weight.T, value_weight.T, out_weight], axis=0)
-    full = gather(packed, "batch", "ctx", 0).reshape(shards, packed.shape[0], width)
+    packed = jnp.pad(packed, ((0, -packed.shape[0] % (16 * size_h)), (0, 0)))
+    full = gather_weights(packed.reshape(size_h, -1, width), 0).reshape(shards, -1, width)
     full_q = full[:, :n_q].reshape(-1, width)
     full_k = full[:, n_q : n_q + n_k].reshape(-1, width)
     full_v = full[:, n_q + n_k : n_q + 2 * n_k].reshape(-1, width)
-    full_o = full[:, n_q + 2 * n_k :].reshape(-1, width)
+    full_o = full[:, n_q + 2 * n_k : n_q + 2 * n_k + n_o].reshape(-1, width)
 
     inputs = tokens[0].astype(jnp.float32)
     first_pos = (ctx_index * size_h + head_index) * tok
@@ -391,7 +614,8 @@
     )
     gain_flat = jnp.concatenate(gains)
     gain_rows = -(-gain_flat.shape[0] // width)
-    gain_pad = -(-gain_rows // 16) * 16
+    fixed = n_q + 2 * n_k + n_o
+    gain_pad = gain_rows + -(fixed + gain_rows) % 32
     gain_block = jnp.pad(gain_flat, (0, gain_pad * width - gain_flat.shape[0])).astype(low)
     gain_block = jnp.broadcast_to(gain_block.reshape(1, gain_pad, width), (shards, gain_pad, width))
     split = (
@@ -402,16 +626,14 @@
         gain_block,
     )
     grads = jnp.concatenate(split, axis=1)
-    depth = grads.shape[1]
-    summed = scatter_sum(
-        grads.reshape(size_b, size_c, depth, width), "batch", "ctx", 7, low
-    )
-    stacked = jnp.concatenate([summed, gate_w_grad, up_w_grad, down_grad], axis=0)
-    unit = 16 * size_h
-    used = stacked.shape[0]
-    stacked = jnp.pad(stacked, ((0, -used % unit), (0, 0)))
-    done = total_over(stacked.reshape(size_h, -1, width), "head", 8)
-    done = done.reshape(-1, width).astype(jnp.float32)
+    wide = jnp.concatenate([gate_w_grad, up_w_grad, down_grad], axis=0)
+    wide = jnp.pad(wide, ((0, -wide.shape[0] % (16 * size_h)), (0, 0)))
+    done, wide_done = sum_grads(
+        grads.reshape(size_b, size_c, 2, -1, width), wide.reshape(size_h, -1, width), 7
+    )
+    done = jnp.concatenate(
+        [done.reshape(-1, width), wide_done.reshape(-1, width)], axis=0
+    ).astype(jnp.float32)
 
     parts = []
     start = 0

time: 325 us -> 248 us (0.76)
  Pallas kernels: 269 us -> 193 us
  matrix products: 20.5 us -> 15.8 us
  other arithmetic: 11.3 us -> 15.1 us
    pallas_call x4 -> x3, Pallas kernels: 120 us -> 64.2 us  [scatter_sum(): pl.pallas_call(functools.partial(scatter_kernel, first, second), out_shap...]
    pallas_call x4 -> x3, Pallas kernels: 113 us -> 58.5 us  [gather(): pl.pallas_call(functools.partial(gather_kernel, first, second), out_shape...]
    pallas_call x1 -> x2, Pallas kernels: 35.8 us -> 69.8 us  [the longest x1 41.7 us: sum_grads(): pl.pallas_call(grads_kernel, out_shape=(jax.ShapeDtypeStruct((2,) + block...]
    unnamed x119 -> x91, local copies, waits for them, and re-layouts: 11.3 us -> 12.6 us
where the time goes in v2:
time: 248 us; the launch traced here: 247 us
  Pallas kernels  193 us (78%)
  local copies, waits for them, and re-layouts  22.3 us (9%)
  matrix products  15.8 us (6%)
  other arithmetic  15.1 us (6%)
    pallas_call x3, Pallas kernels, scatter_sum(): pl.pallas_call(functools.partial(scatter_kernel, first, second), out_shap...  64.2 us
    pallas_call x3, Pallas kernels, gather(): pl.pallas_call(functools.partial(gather_kernel, first, second), out_shape...  58.5 us
    pallas_call x1, Pallas kernels, sum_grads(): pl.pallas_call(grads_kernel, out_shape=(jax.ShapeDtypeStruct((2,) + block...  41.7 us
    pallas_call x1, Pallas kernels, gather_weights(): pl.pallas_call(weights_kernel, out_shape=jax.ShapeDtypeStruct((size_a, si...  28.1 us
    unnamed x91, local copies, waits for them, and re-layouts  12.6 us
    dot_general x9, matrix products, contract_cols(): lax.dot_general(left, right, (((1,), (1,)), ((), ())), preferred_element_...  5.58 us

profile of v2, /device:TPU:9, one launch (start us, length us, event | category | flops | bytes accessed | tf_op | source)
XLA Modules:
  0.0 247.3 jit_solution(5469101542268503466)
XLA Ops:
  0.7 1.1 fusion.29
  1.7 0.5 copy-done.34
  2.3 1.1 copy.36
  3.3 1.0 pad_maximum_fusion.2
  4.3 28.1 %gather_weights.1 = bf16[4,2,4,80,640]{4,3,2,1,0:T(8,128)(2,1)} custom-call(bf16[4,80,640]{2,1,0:T(8,128)(2,1)S(1)} %bitcast.169), custom_call_target="tpu_custom_call" | custom-call | tf_op jit(solution)/shard_map/gather_weights/pallas_call | solution.py:294
  32.4 1.1 fusion.77
  33.6 0.7 copy-done.16
  34.3 0.3 multiply_reduce_fusion.13
  35.1 3.1 %fusion.76 = (bf16[8,128,640]{2,1,0:T(8,128)(2,1)}, bf16[8,128,640]{2,1,0:T(8,128)(2,1)S(1)}) fusion(bf16[8,320,640]{2,1,0:T(8,128)(2,1)} %bitcast.177), kind=kLoop, calls=%fused_computation.170 | loop fusion | bytes 5242880 | tf_op jit(solution)/shard_map/slice | solution.py:502
  38.3 0.7 multiply_reduce_fusion.3
  39.3 0.4 copy-done.6
  40.0 13.9 %gather_ctx_head.1 = bf16[2,4,128,512]{3,2,1,0:T(8,128)(2,1)S(1)} custom-call(bf16[128,512]{1,0:T(8,128)(2,1)S(1)} %pad_maximum_fusion.5.x_ref), custom_call_target="tpu_custom_call" | custom-call | tf_op jit(solution)/shard_map/gather_ctx_head/pallas_call | solution.py:120
  53.9 0.6 fusion
  54.5 0.7 fusion.74
  55.3 1.7 fusion.80
  57.0 1.1 copy.37
  58.1 0.5 multiply_reduce_fusion.10
  59.0 24.2 %gather_batch_ctx.2 = bf16[4,2,128,640]{3,2,1,0:T(8,128)(2,1)S(1)} custom-call(bf16[128,640]{1,0:T(8,128)(2,1)S(1)} %multiply_convert_fusion.4.x_ref), custom_call_target="tpu_custom_call" | custom-call | tf_op jit(solution)/shard_map/gather_batch_ctx/pallas_call | solution.py:120
  83.2 0.6 fusion.81
  83.8 0.6 multiply_convert_fusion.3
  84.5 0.6 convolution_convert_fusion
  85.0 26.6 %scatter_batch_ctx.2 = f32[128,640]{1,0:T(8,128)S(1)} custom-call(bf16[4,2,128,640]{3,2,1,0:T(8,128)(2,1)S(1)} %bitcast.167), custom_call_target="tpu_custom_call" | custom-call | tf_op jit(solution)/shard_map/scatter_batch_ctx/pallas_call | solution.py:180
  111.9 0.8 fusion.33
  112.8 20.4 %gather_batch_ctx.3 = bf16[4,2,128,640]{3,2,1,0:T(8,128)(2,1)S(1)} custom-call(bf16[128,640]{1,0:T(8,128)(2,1)S(1)} %get-tuple-element.82.x_ref), custom_call_target="tpu_custom_call" | custom-call | tf_op jit(solution)/shard_map/gather_batch_ctx/pallas_call | solution.py:120
  133.2 0.6 convolution_convert_fusion.4
  133.8 1.1 multiply_convert_fusion.2
  135.0 0.6 convolution_convert_fusion.5
  135.6 0.6 convolution_convert_fusion.6
  136.2 1.1 pad_maximum_fusion.1
  137.3 0.6 fusion.82
  137.9 0.6 add_convert_fusion
  138.5 19.9 %scatter_batch_ctx.3 = f32[128,640]{1,0:T(8,128)S(1)} custom-call(bf16[4,2,128,640]{3,2,1,0:T(8,128)(2,1)S(1)} %bitcast.162), custom_call_target="tpu_custom_call" | custom-call | tf_op jit(solution)/shard_map/scatter_batch_ctx/pallas_call | solution.py:180
  159.1 0.5 convolution_convert_fusion.9
  159.8 0.8 copy-done.12
  160.6 0.8 multiply_convert_fusion
  161.5 1.0 copy-done.37
  162.4 0.5 fusion.1
  162.9 0.9 convolution_convert_fusion.3
  163.8 1.1 pad_maximum_fusion
  164.9 1.5 copy.40
  166.4 17.7 %scatter_ctx_head.1 = f32[128,512]{1,0:T(8,128)S(1)} custom-call(bf16[2,4,128,512]{3,2,1,0:T(8,128)(2,1)S(1)} %bitcast.168), custom_call_target="tpu_custom_call" | custom-call | tf_op jit(solution)/shard_map/scatter_ctx_head/pallas_call | solution.py:180
  184.6 0.7 multiply_multiply_fusion.7
  185.3 0.7 fusion.46
  186.1 0.4 fusion.2
  186.6 0.5 copy-done.7
  187.4 0.9 fusion.10
  188.3 1.2 copy.39
  189.5 0.4 fusion.83
  190.1 0.3 fusion.28
  191.5 0.4 dynamic-update-slice.10
  192.0 0.6 convolution_convert_fusion.2
  193.5 0.5 convolution_convert_fusion.1
  194.3 1.8 copy-done.8
  196.1 41.7 %sum_grads.1 = (bf16[2,176,640]{2,1,0:T(8,128)(2,1)S(1)}, bf16[4,192,640]{2,1,0:T(8,128)(2,1)S(1)}) custom-call(bf16[4,2,2,176,640]{4,3,2,1,0:T(8,128)(2,1)} %bitcast.182, bf16[4,192,640]{2,1,0:T(8,128)(2,1)} %bitcast.185), custom_call_target="tpu_custom_call" | custom-call | tf_op jit(solution)/shard_map/sum_grads/pallas_call | solution.py:433
  237.8 1.2 fusion.38
  239.0 2.2 copy.42
  241.2 1.1 copy.43
  242.2 0.7 maximum_convert_fusion.1
  242.9 0.6 fusion.78
  243.5 0.6 fusion.79
  244.1 0.8 maximum_convert_fusion
  244.9 0.9 copy.41
  245.8 0.6 convert_reduce_fusion
  246.4 0.9 fusion.36
  (124 shorter events, 6.0 us)
Async XLA Ops:
  0.6 83.8 %copy-start = (bf16[256,640]{1,0:T(8,128)(2,1)S(1)}, bf16[256,640]{1,0:T(8,128)(2,1)}, u32[]{:S(2)}) copy-start(bf16[256,640]{1,0:T(8,128)(2,1)} %param.27) | copy-start | bytes 983044
  1.7 0.5 copy-start.34
  4.3 30.0 %copy-start.5 = (bf16[1,128,640]{2,1,0:T(8,128)(2,1)S(1)}, bf16[1,128,640]{2,1,0:T(8,128)(2,1)}, u32[]{:S(2)}) copy-start(bf16[1,128,640]{2,1,0:T(8,128)(2,1)} %param.15) | copy-start | bytes 491524
  4.3 30.0 %copy-start.28 = (f32[640]{0:T(1024)S(1)}, f32[640]{0:T(1024)}, u32[]{:S(2)}) copy-start(f32[640]{0:T(1024)} %param.16) | copy-start | bytes 7684
  4.3 30.3 %copy-start.32 = (f32[256]{0:T(256)S(1)}, f32[256]{0:T(256)}, u32[]{:S(2)}) copy-start(f32[256]{0:T(256)} %param.21) | copy-start | bytes 3076
  33.6 0.7 copy-start.16
  33.6 5.8 %copy-start.18 = (bf16[8,32,640]{2,1,0:T(8,128)(2,1)}, bf16[8,32,640]{2,1,0:T(8,128)(2,1)S(1)}, u32[]{:S(2)}) copy-start(bf16[8,32,640]{2,1,0:T(8,128)(2,1)S(1)} %get-tuple-element.67) | copy-start | bytes 983044
  34.6 3.6 %copy-start.36 = (f32[128]{0:T(128)}, f32[128]{0:T(128)S(1)}, u32[]{:S(2)}) copy-start(f32[128]{0:T(128)S(1)} %get-tuple-element.97) | copy-start | bytes 1540
  35.1 4.0 %copy-start.21 = (f32[128,128]{1,0:T(8,128)}, f32[128,128]{1,0:T(8,128)S(1)}, u32[]{:S(2)}) copy-start(f32[128,128]{1,0:T(8,128)S(1)} %get-tuple-element.94) | copy-start | bytes 196612
  35.1 3.8 %copy-start.33 = (f32[256]{0:T(256)S(1)}, f32[256]{0:T(256)}, u32[]{:S(2)}) copy-start(f32[256]{0:T(256)} %param.20) | copy-start | bytes 3076
  38.3 1.1 copy-start.3
  38.9 0.8 copy-start.6
  39.3 15.2 %copy-start.26 = (bf16[128,4,256]{2,0,1:T(8,128)(2,1)}, bf16[128,4,256]{2,0,1:T(8,128)(2,1)S(1)}, u32[]{:S(2)}) copy-start(bf16[128,4,256]{2,0,1:T(8,128)(2,1)S(1)} %pad_maximum_fusion.4) | copy-start | bytes 786436
  54.5 2.4 copy-start.11
  55.3 2.9 %copy-start.1 = (bf16[8,128,640]{2,1,0:T(8,128)(2,1)S(1)}, bf16[8,128,640]{2,1,0:T(8,128)(2,1)}, u32[]{:S(2)}) copy-start(bf16[8,128,640]{2,1,0:T(8,128)(2,1)} %get-tuple-element.64) | copy-start | bytes 3932164
  57.0 1.7 copy-start.29
  57.0 1.9 copy-start.30
  58.1 25.1 %copy-start.9 = (bf16[4,128,256]{1,2,0:T(8,128)(2,1)}, bf16[4,128,256]{1,2,0:T(8,128)(2,1)S(1)}, u32[]{:S(2)}) copy-start(bf16[4,128,256]{1,2,0:T(8,128)(2,1)S(1)} %copy.37) | copy-start | bytes 786436
  58.1 25.1 %copy-start.20 = (bf16[640,256]{1,0:T(8,128)(2,1)S(1)}, bf16[640,256]{1,0:T(8,128)(2,1)}, u32[]{:S(2)}) copy-start(bf16[640,256]{1,0:T(8,128)(2,1)} %param.25) | copy-start | bytes 983044
  59.0 24.8 %copy-start.25 = (bf16[640,256]{1,0:T(8,128)(2,1)S(1)}, bf16[640,256]{1,0:T(8,128)(2,1)}, u32[]{:S(2)}) copy-start(bf16[640,256]{1,0:T(8,128)(2,1)} %param.26) | copy-start | bytes 983044
  84.4 27.3 %copy-start.13 = (bf16[1,128,640]{2,1,0:T(8,128)(2,1)S(1)}, bf16[1,128,640]{2,1,0:T(8,128)(2,1)}, u32[]{:S(2)}) copy-start(bf16[1,128,640]{2,1,0:T(8,128)(2,1)} %param.29) | copy-start | bytes 491524
  84.4 27.3 %copy-start.31 = (f32[640]{0:T(1024)S(1)}, f32[640]{0:T(1024)}, u32[]{:S(2)}) copy-start(f32[640]{0:T(1024)} %param.28) | copy-start | bytes 7684
  138.5 20.6 %copy-start.2 = (bf16[8,128,640]{2,1,0:T(8,128)(2,1)S(1)}, bf16[8,128,640]{2,1,0:T(8,128)(2,1)}, u32[]{:S(2)}) copy-start(bf16[8,128,640]{2,1,0:T(8,128)(2,1)} %get-tuple-element.64) | copy-start | bytes 3932164
  158.6 1.1 copy-start.24
  158.9 1.7 copy-start.12
  159.0 2.4 copy-start.14
  160.6 1.8 copy-start.27
  161.4 1.0 copy-start.37
  166.4 19.6 %copy-start.38 = (bf16[512,1024]{1,0:T(8,128)(2,1)S(1)}, bf16[512,1024]{1,0:T(8,128)(2,1)}, u32[]{:S(2)}) copy-start(bf16[512,1024]{1,0:T(8,128)(2,1)} %copy-done.37) | copy-start | bytes 3145732
  184.2 2.4 copy-start.22
  186.0 1.0 copy-start.7
  186.5 2.9 %copy-start.4 = (bf16[8,128,640]{2,1,0:T(8,128)(2,1)S(1)}, bf16[8,128,640]{2,1,0:T(8,128)(2,1)}, u32[]{:S(2)}) copy-start(bf16[8,128,640]{2,1,0:T(8,128)(2,1)} %copy-done.3) | copy-start | bytes 3932164
  187.3 2.5 %copy-start.17 = (bf16[8,32,640]{2,1,0:T(8,128)(2,1)S(1)}, bf16[8,32,640]{2,1,0:T(8,128)(2,1)}, u32[]{:S(2)}) copy-start(bf16[8,32,640]{2,1,0:T(8,128)(2,1)} %copy-done.16) | copy-start | bytes 983044
  187.3 2.5 %copy-start.23 = (bf16[128,256]{1,0:T(8,128)(2,1)S(1)}, bf16[128,256]{1,0:T(8,128)(2,1)}, u32[]{:S(2)}) copy-start(bf16[128,256]{1,0:T(8,128)(2,1)} %fusion.46) | copy-start | bytes 196612
  188.3 1.8 copy-start.19
  192.5 1.0 copy-start.10
  192.5 1.0 copy-start.15
  194.3 1.8 copy-start.8
  244.1 2.3 copy-start.35

commit v3 on v2

--- a/solution.py
+++ b/solution.py
@@ -86,31 +86,66 @@
     at_a, at_b = lax.axis_index(first), lax.axis_index(second)
     greet((first, second))
     own = out_ref.at[at_a, at_b]
-    sent_a, sent_b = [], []
-    for step in range(1, size_a):
-        sent_a.append(
-            send(x_ref, own, send_a.at[step - 1], recv_a.at[step - 1], first,
-                 lax.rem(at_a + step, size_a))
-        )
-    for turn in range(1, size_b):
-        sent_b.append(
-            send(x_ref, own, send_b.at[turn - 1, 0], recv_b.at[turn - 1, 0], second,
-                 lax.rem(at_b + turn, size_b))
-        )
+
+    def along(source, target, way, step, goal):
+        return pltpu.make_async_remote_copy(
+            src_ref=source,
+            dst_ref=target,
+            send_sem=send_a.at[way, step],
+            recv_sem=recv_a.at[way, step],
+            device_id={first: goal},
+            device_id_type=pl.DeviceIdType.MESH,
+        )
+
+    def across(source, target, way, step):
+        return [
+            pltpu.make_async_remote_copy(
+                src_ref=source,
+                dst_ref=target,
+                send_sem=send_b.at[turn - 1, way, step],
+                recv_sem=recv_b.at[turn - 1, way, step],
+                device_id={second: lax.rem(at_b + turn, size_b)},
+                device_id_type=pl.DeviceIdType.MESH,
+            )
+            for turn in range(1, size_b)
+        ]
+
+    ups = at_a < size_a - 1
+    downs = at_a > 0
+    ahead = lax.rem(at_a + 1, size_a)
+    behind = lax.rem(at_a + size_a - 1, size_a)
+    pl.when(ups)(lambda: along(x_ref, own, 0, 0, ahead).start())
+    pl.when(downs)(lambda: along(x_ref, own, 1, 0, behind).start())
+    for copy in across(x_ref, own, 0, 0):
+        copy.start()
     keep = pltpu.make_async_copy(x_ref, own, own_sem)
     keep.start()
-    for step in range(1, size_a):
-        sent_a[step - 1].wait_recv()
-        slot = out_ref.at[lax.rem(at_a + size_a - step, size_a), at_b]
-        for turn in range(1, size_b):
-            sent_b.append(
-                send(slot, slot, send_b.at[turn - 1, step], recv_b.at[turn - 1, step], second,
-                     lax.rem(at_b + turn, size_b))
-            )
-    for copy in sent_b:
-        copy.wait_recv()
-    for copy in sent_a + sent_b:
-        copy.wait_send()
+
+    def hand_on(way, step):
+        source = at_a - step if way == 0 else at_a + step
+        slot = out_ref.at[source, at_b]
+        goal = ahead if way == 0 else behind
+        along(slot, slot, way, step - 1, goal).wait_recv()
+        pl.when(ups if way == 0 else downs)(lambda: along(slot, slot, way, step, goal).start())
+        for copy in across(slot, slot, way, step):
+            copy.start()
+
+    def finish(way, step):
+        source = at_a - step if way == 0 else at_a + step
+        slot = out_ref.at[source, at_b]
+        goal = ahead if way == 0 else behind
+        for copy in across(slot, slot, way, step):
+            copy.wait()
+        pl.when(ups if way == 0 else downs)(lambda: along(slot, slot, way, step, goal).wait_send())
+
+    for stage in (hand_on, finish):
+        for step in range(1, size_a):
+            pl.when(at_a >= step)(functools.partial(stage, 0, step))
+            pl.when(at_a < size_a - step)(functools.partial(stage, 1, step))
+    for copy in across(x_ref, own, 0, 0):
+        copy.wait()
+    pl.when(ups)(lambda: along(x_ref, own, 0, 0, ahead).wait_send())
+    pl.when(downs)(lambda: along(x_ref, own, 1, 0, behind).wait_send())
     keep.wait()
 
 
@@ -122,13 +157,9 @@
         out_shape=jax.ShapeDtypeStruct((size_a, size_b) + values.shape, values.dtype),
         in_specs=[pl.BlockSpec(memory_space=pl.ANY)],
         out_specs=pl.BlockSpec(memory_space=pl.ANY),
-        scratch_shapes=[
-            dma,
-            dma((size_a - 1,)),
-            dma((size_a - 1,)),
-            dma((size_b - 1, size_a)),
-            dma((size_b - 1, size_a)),
-        ],
+        scratch_shapes=[dma]
+        + [dma((2, size_a))] * 2
+        + [dma((size_b - 1, 2, size_a))] * 2,
         compiler_params=pltpu.CompilerParams(
             collective_id=number, has_side_effects=True, vmem_limit_bytes=vmem_limit
         ),

time: 248 us -> 239 us (0.964)
  Pallas kernels: 193 us -> 184 us
    pallas_call x3, Pallas kernels: 58.5 us -> 53.1 us  [gather(): pl.pallas_call(functools.partial(gather_kernel, first, second), out_shape...]
    pallas_call x3, Pallas kernels: 64.2 us -> 61.3 us  [scatter_sum(): pl.pallas_call(functools.partial(scatter_kernel, first, second), out_shap...]
where the time goes in v3:
time: 239 us
  Pallas kernels  184 us (77%)
  local copies, waits for them, and re-layouts  22.3 us (9%)
  matrix products  15.7 us (7%)
  other arithmetic  15.1 us (6%)
    pallas_call x3, Pallas kernels, scatter_sum(): pl.pallas_call(functools.partial(scatter_kernel, first, second), out_shap...  61.3 us
    pallas_call x3, Pallas kernels, gather(): pl.pallas_call(functools.partial(gather_kernel, first, second), out_shape...  53.1 us
    pallas_call x1, Pallas kernels, sum_grads(): pl.pallas_call(grads_kernel, out_shape=(jax.ShapeDtypeStruct((2,) + block...  41.6 us
    pallas_call x1, Pallas kernels, gather_weights(): pl.pallas_call(weights_kernel, out_shape=jax.ShapeDtypeStruct((size_a, si...  28.1 us
    unnamed x91, local copies, waits for them, and re-layouts  12.6 us
    dot_general x9, matrix products, contract_cols(): lax.dot_general(left, right, (((1,), (1,)), ((), ())), preferred_element_...  5.58 us
    dot_general x9, matrix products, contract_rows(): lax.dot_general(left, right, (((0,), (0,)), ((), ())), preferred_element_...  4.85 us

profile of v3, /device:TPU:9, one launch (start us, length us, event | category | flops | bytes accessed | tf_op | source)
XLA Modules:
  0.0 238.8 jit_solution(6953881328783785278)
XLA Ops:
  0.7 1.1 fusion.29
  1.7 0.5 copy-done.34
  2.3 1.1 copy.36
  3.3 1.0 pad_maximum_fusion.2
  4.3 28.1 %gather_weights.1 = bf16[4,2,4,80,640]{4,3,2,1,0:T(8,128)(2,1)} custom-call(bf16[4,80,640]{2,1,0:T(8,128)(2,1)S(1)} %bitcast.169), custom_call_target="tpu_custom_call" | custom-call | tf_op jit(solution)/shard_map/gather_weights/pallas_call | solution.py:325
  32.4 1.1 fusion.77
  33.6 0.7 copy-done.16
  34.3 0.3 multiply_reduce_fusion.13
  35.1 3.1 %fusion.76 = (bf16[8,128,640]{2,1,0:T(8,128)(2,1)}, bf16[8,128,640]{2,1,0:T(8,128)(2,1)S(1)}) fusion(bf16[8,320,640]{2,1,0:T(8,128)(2,1)} %bitcast.177), kind=kLoop, calls=%fused_computation.170 | loop fusion | bytes 5242880 | tf_op jit(solution)/shard_map/slice | solution.py:533
  38.3 0.7 multiply_reduce_fusion.3
  39.3 0.4 copy-done.6
  40.0 14.1 %gather_ctx_head.1 = bf16[2,4,128,512]{3,2,1,0:T(8,128)(2,1)S(1)} custom-call(bf16[128,512]{1,0:T(8,128)(2,1)S(1)} %pad_maximum_fusion.5.x_ref), custom_call_target="tpu_custom_call" | custom-call | tf_op jit(solution)/shard_map/gather_ctx_head/pallas_call | solution.py:155
  54.1 0.6 fusion
  54.7 0.7 fusion.74
  55.4 1.7 fusion.80
  57.1 1.1 copy.37
  58.3 0.5 multiply_reduce_fusion.10
  59.2 21.9 %gather_batch_ctx.2 = bf16[4,2,128,640]{3,2,1,0:T(8,128)(2,1)S(1)} custom-call(bf16[128,640]{1,0:T(8,128)(2,1)S(1)} %multiply_convert_fusion.4.x_ref), custom_call_target="tpu_custom_call" | custom-call | tf_op jit(solution)/shard_map/gather_batch_ctx/pallas_call | solution.py:155
  81.1 0.6 fusion.81
  81.7 0.6 multiply_convert_fusion.3
  82.3 0.6 convolution_convert_fusion
  82.9 21.2 %scatter_batch_ctx.2 = f32[128,640]{1,0:T(8,128)S(1)} custom-call(bf16[4,2,128,640]{3,2,1,0:T(8,128)(2,1)S(1)} %bitcast.167), custom_call_target="tpu_custom_call" | custom-call | tf_op jit(solution)/shard_map/scatter_batch_ctx/pallas_call | solution.py:211
  104.5 0.8 fusion.33
  105.3 17.2 %gather_batch_ctx.3 = bf16[4,2,128,640]{3,2,1,0:T(8,128)(2,1)S(1)} custom-call(bf16[128,640]{1,0:T(8,128)(2,1)S(1)} %get-tuple-element.82.x_ref), custom_call_target="tpu_custom_call" | custom-call | tf_op jit(solution)/shard_map/gather_batch_ctx/pallas_call | solution.py:155
  122.5 0.6 convolution_convert_fusion.4
  123.1 1.1 multiply_convert_fusion.2
  124.2 0.6 convolution_convert_fusion.5
  124.8 0.6 convolution_convert_fusion.6
  125.4 1.1 pad_maximum_fusion.1
  126.5 0.6 fusion.82
  127.1 0.6 add_convert_fusion
  127.7 19.2 %scatter_batch_ctx.3 = f32[128,640]{1,0:T(8,128)S(1)} custom-call(bf16[4,2,128,640]{3,2,1,0:T(8,128)(2,1)S(1)} %bitcast.162), custom_call_target="tpu_custom_call" | custom-call | tf_op jit(solution)/shard_map/scatter_batch_ctx/pallas_call | solution.py:211
  147.6 0.5 convolution_convert_fusion.9
  148.3 0.8 copy-done.12
  149.1 0.8 multiply_convert_fusion
  150.0 1.0 copy-done.37
  150.9 0.5 fusion.1
  151.4 0.9 convolution_convert_fusion.3
  152.4 1.1 pad_maximum_fusion
  153.5 1.5 copy.40
  155.0 20.8 %scatter_ctx_head.1 = f32[128,512]{1,0:T(8,128)S(1)} custom-call(bf16[2,4,128,512]{3,2,1,0:T(8,128)(2,1)S(1)} %bitcast.168), custom_call_target="tpu_custom_call" | custom-call | tf_op jit(solution)/shard_map/scatter_ctx_head/pallas_call | solution.py:211
  176.3 0.7 multiply_multiply_fusion.7
  177.0 0.7 fusion.46
  177.7 0.4 fusion.2
  178.3 0.5 copy-done.7
  179.0 0.9 fusion.10
  179.9 1.2 copy.39
  181.1 0.4 fusion.83
  181.8 0.3 fusion.28
  183.2 0.4 dynamic-update-slice.10
  183.6 0.6 convolution_convert_fusion.2
  185.2 0.5 convolution_convert_fusion.1
  186.0 1.8 copy-done.8
  187.7 41.6 %sum_grads.1 = (bf16[2,176,640]{2,1,0:T(8,128)(2,1)S(1)}, bf16[4,192,640]{2,1,0:T(8,128)(2,1)S(1)}) custom-call(bf16[4,2,2,176,640]{4,3,2,1,0:T(8,128)(2,1)} %bitcast.182, bf16[4,192,640]{2,1,0:T(8,128)(2,1)} %bitcast.185), custom_call_target="tpu_custom_call" | custom-call | tf_op jit(solution)/shard_map/sum_grads/pallas_call | solution.py:464
  229.3 1.2 fusion.38
  230.5 2.2 copy.42
  232.7 1.1 copy.43
  233.8 0.7 maximum_convert_fusion.1
  234.4 0.6 fusion.78
  235.0 0.6 fusion.79
  235.6 0.8 maximum_convert_fusion
  236.4 0.9 copy.41
  237.3 0.6 convert_reduce_fusion
  237.9 0.9 fusion.36
  (124 shorter events, 6.0 us)
Async XLA Ops:
  0.6 81.7 %copy-start = (bf16[256,640]{1,0:T(8,128)(2,1)S(1)}, bf16[256,640]{1,0:T(8,128)(2,1)}, u32[]{:S(2)}) copy-start(bf16[256,640]{1,0:T(8,128)(2,1)} %param.27) | copy-start | bytes 983044
  1.7 0.5 copy-start.34
  4.3 30.0 %copy-start.5 = (bf16[1,128,640]{2,1,0:T(8,128)(2,1)S(1)}, bf16[1,128,640]{2,1,0:T(8,128)(2,1)}, u32[]{:S(2)}) copy-start(bf16[1,128,640]{2,1,0:T(8,128)(2,1)} %param.15) | copy-start | bytes 491524
  4.3 30.0 %copy-start.28 = (f32[640]{0:T(1024)S(1)}, f32[640]{0:T(1024)}, u32[]{:S(2)}) copy-start(f32[640]{0:T(1024)} %param.16) | copy-start | bytes 7684
  4.3 30.3 %copy-start.32 = (f32[256]{0:T(256)S(1)}, f32[256]{0:T(256)}, u32[]{:S(2)}) copy-start(f32[256]{0:T(256)} %param.21) | copy-start | bytes 3076
  33.6 0.7 copy-start.16
  33.6 5.8 %copy-start.18 = (bf16[8,32,640]{2,1,0:T(8,128)(2,1)}, bf16[8,32,640]{2,1,0:T(8,128)(2,1)S(1)}, u32[]{:S(2)}) copy-start(bf16[8,32,640]{2,1,0:T(8,128)(2,1)S(1)} %get-tuple-element.67) | copy-start | bytes 983044
  34.6 3.6 %copy-start.36 = (f32[128]{0:T(128)}, f32[128]{0:T(128)S(1)}, u32[]{:S(2)}) copy-start(f32[128]{0:T(128)S(1)} %get-tuple-element.97) | copy-start | bytes 1540
  35.1 4.0 %copy-start.21 = (f32[128,128]{1,0:T(8,128)}, f32[128,128]{1,0:T(8,128)S(1)}, u32[]{:S(2)}) copy-start(f32[128,128]{1,0:T(8,128)S(1)} %get-tuple-element.94) | copy-start | bytes 196612
  35.1 3.8 %copy-start.33 = (f32[256]{0:T(256)S(1)}, f32[256]{0:T(256)}, u32[]{:S(2)}) copy-start(f32[256]{0:T(256)} %param.20) | copy-start | bytes 3076
  38.3 1.1 copy-start.3
  38.9 0.8 copy-start.6
  39.3 15.3 %copy-start.26 = (bf16[128,4,256]{2,0,1:T(8,128)(2,1)}, bf16[128,4,256]{2,0,1:T(8,128)(2,1)S(1)}, u32[]{:S(2)}) copy-start(bf16[128,4,256]{2,0,1:T(8,128)(2,1)S(1)} %pad_maximum_fusion.4) | copy-start | bytes 786436
  54.7 2.4 %copy-start.11 = (f32[512,1024]{1,0:T(8,128)}, f32[512,1024]{1,0:T(8,128)S(1)}, u32[]{:S(2)}) copy-start(f32[512,1024]{1,0:T(8,128)S(1)} %get-tuple-element.102) | copy-start | bytes 6291460
  55.4 2.9 %copy-start.1 = (bf16[8,128,640]{2,1,0:T(8,128)(2,1)S(1)}, bf16[8,128,640]{2,1,0:T(8,128)(2,1)}, u32[]{:S(2)}) copy-start(bf16[8,128,640]{2,1,0:T(8,128)(2,1)} %get-tuple-element.64) | copy-start | bytes 3932164
  57.1 1.7 copy-start.29
  57.1 1.9 copy-start.30
  58.3 22.8 %copy-start.9 = (bf16[4,128,256]{1,2,0:T(8,128)(2,1)}, bf16[4,128,256]{1,2,0:T(8,128)(2,1)S(1)}, u32[]{:S(2)}) copy-start(bf16[4,128,256]{1,2,0:T(8,128)(2,1)S(1)} %copy.37) | copy-start | bytes 786436
  58.3 22.8 %copy-start.20 = (bf16[640,256]{1,0:T(8,128)(2,1)S(1)}, bf16[640,256]{1,0:T(8,128)(2,1)}, u32[]{:S(2)}) copy-start(bf16[640,256]{1,0:T(8,128)(2,1)} %param.25) | copy-start | bytes 983044
  59.2 22.5 %copy-start.25 = (bf16[640,256]{1,0:T(8,128)(2,1)S(1)}, bf16[640,256]{1,0:T(8,128)(2,1)}, u32[]{:S(2)}) copy-start(bf16[640,256]{1,0:T(8,128)(2,1)} %param.26) | copy-start | bytes 983044
  82.3 22.0 %copy-start.13 = (bf16[1,128,640]{2,1,0:T(8,128)(2,1)S(1)}, bf16[1,128,640]{2,1,0:T(8,128)(2,1)}, u32[]{:S(2)}) copy-start(bf16[1,128,640]{2,1,0:T(8,128)(2,1)} %param.29) | copy-start | bytes 491524
  82.3 22.0 %copy-start.31 = (f32[640]{0:T(1024)S(1)}, f32[640]{0:T(1024)}, u32[]{:S(2)}) copy-start(f32[640]{0:T(1024)} %param.28) | copy-start | bytes 7684
  127.7 19.8 %copy-start.2 = (bf16[8,128,640]{2,1,0:T(8,128)(2,1)S(1)}, bf16[8,128,640]{2,1,0:T(8,128)(2,1)}, u32[]{:S(2)}) copy-start(bf16[8,128,640]{2,1,0:T(8,128)(2,1)} %get-tuple-element.64) | copy-start | bytes 3932164
  147.1 1.1 copy-start.24
  147.4 1.7 copy-start.12
  147.6 2.4 copy-start.14
  149.1 1.8 copy-start.27
  150.0 1.0 copy-start.37
  155.0 22.7 %copy-start.38 = (bf16[512,1024]{1,0:T(8,128)(2,1)S(1)}, bf16[512,1024]{1,0:T(8,128)(2,1)}, u32[]{:S(2)}) copy-start(bf16[512,1024]{1,0:T(8,128)(2,1)} %copy-done.37) | copy-start | bytes 3145732
  175.8 2.4 %copy-start.22 = (f32[128,128]{1,0:T(8,128)S(1)}, f32[128,128]{1,0:T(8,128)}, u32[]{:S(2)}) copy-start(f32[128,128]{1,0:T(8,128)} %copy-done.21) | copy-start | bytes 196612
  177.7 1.0 copy-start.7
  178.2 2.9 %copy-start.4 = (bf16[8,128,640]{2,1,0:T(8,128)(2,1)S(1)}, bf16[8,128,640]{2,1,0:T(8,128)(2,1)}, u32[]{:S(2)}) copy-start(bf16[8,128,640]{2,1,0:T(8,128)(2,1)} %copy-done.3) | copy-start | bytes 3932164
  179.0 2.5 %copy-start.17 = (bf16[8,32,640]{2,1,0:T(8,128)(2,1)S(1)}, bf16[8,32,640]{2,1,0:T(8,128)(2,1)}, u32[]{:S(2)}) copy-start(bf16[8,32,640]{2,1,0:T(8,128)(2,1)} %copy-done.16) | copy-start | bytes 983044
  179.0 2.5 %copy-start.23 = (bf16[128,256]{1,0:T(8,128)(2,1)S(1)}, bf16[128,256]{1,0:T(8,128)(2,1)}, u32[]{:S(2)}) copy-start(bf16[128,256]{1,0:T(8,128)(2,1)} %fusion.46) | copy-start | bytes 196612
  179.9 1.8 copy-start.19
  184.2 1.0 copy-start.10
  184.2 1.0 copy-start.15
  186.0 1.8 copy-start.8
  235.6 2.3 copy-start.35
